TPU v7x, 512 devices: a whole 4x4x16 slice. The times are simulated.
512 devices in a mesh: seq: 64 (over x_lo, z, core), exp: 8 (over x_hi, y).
Axes of the slice: x: 4 (x_hi: 2, x_lo: 2; x = x_hi * 2 + x_lo), y: 4, z: 16, core: 2. Of those that a mesh axis runs over, the one named last changes fastest.
Arguments:
- tokens: bfloat16 [16384, 2048], P('seq', 'exp'), may hold values from -11 to 11
- cotangent: bfloat16 [16384, 2048], P('seq', 'exp'), may hold values from -6 to 6
- slot_keys: bfloat16 [2048, 16], P(None, 'exp'), may hold values from -1 to 1
- expert_in: bfloat16 [16, 2048, 8192], P('exp', None, 'seq'), may hold values from -0.125 to 0.125
- expert_out: bfloat16 [16, 8192, 2048], P('exp', 'seq'), may hold values from -0.0625 to 0.0625
Outputs:
- token_grad: bfloat16 [16384, 2048], P('seq', 'exp')
- key_grad: float32 [2048, 16], P('seq', 'exp')
- in_grad: bfloat16 [16, 2048, 8192], P('exp', None, 'seq')
- out_grad: bfloat16 [16, 8192, 2048], P('exp', 'seq')
All inputs are finite; a program needn't handle non-finite values.
Results may differ from a plain program's by a relative error of at most 0.018.
Values may be sent and summed in bfloat16 or wider, within the bound.
A program may use at most 64 MiB of HBM per device.

v0:
```python
import jax
import jax.numpy as jnp
from jax import lax
from jax.sharding import PartitionSpec as P


def combined_all(value, axis, join):
    pieces = jax.tree.map(lambda part: lax.all_gather(part, axis), value)
    head = jax.tree.map(lambda part: part[0], pieces)
    tail = jax.tree.map(lambda part: part[1:], pieces)
    running, _ = lax.scan(lambda running, piece: (join(running, piece), None), head, tail)
    return running


def gelu_tanh(values):
    return jax.nn.gelu(values, approximate=True)


def merge_stats(first, second):
    peak = jnp.maximum(first[0], second[0])
    total = first[1] * jnp.exp(first[0] - peak) + second[1] * jnp.exp(second[0] - peak)
    return (peak, total)


def column_stats(logits):
    col_peak = lax.pmax(jnp.max(logits, axis=0), "seq")
    col_exp = jnp.exp(logits - col_peak[None, :])
    col_total = lax.psum(jnp.sum(col_exp, axis=0), "seq")
    return (col_peak, col_total)


def column_back(dispatch, grad_dispatch):
    dispatch_col = lax.psum(jnp.sum(dispatch * grad_dispatch, axis=0), "seq")
    return dispatch * (grad_dispatch - dispatch_col[None, :])


def key_total(key_part):
    return lax.psum_scatter(key_part, "seq", scatter_dimension=0, tiled=True)


def per_device(tokens, cotangent, slot_keys, expert_in, expert_out):
    over_rows = (((0,), (0,)), ((), ()))
    over_cols = (((1,), (1,)), ((), ()))
    tokens_all, cotan_all = (
        lax.all_gather(tokens, "exp", axis=1, tiled=True),
        lax.all_gather(cotangent, "exp", axis=1, tiled=True),
    )
    logits = jnp.dot(tokens_all, slot_keys, preferred_element_type=jnp.float32)
    col_peak, col_total = column_stats(logits)
    local_row = jnp.max(logits, axis=1)
    row_sum = jnp.sum(jnp.exp(logits - local_row[:, None]), axis=1)
    row_peak, row_total = combined_all((local_row, row_sum), "exp", merge_stats)
    dispatch = jnp.exp(logits - col_peak[None, :]) / col_total[None, :]
    combine = jnp.exp(logits - row_peak[:, None]) / row_total[:, None]
    dispatch_b = dispatch.astype(jnp.bfloat16)
    combine_b = combine.astype(jnp.bfloat16)
    slot_part = lax.dot_general(
        dispatch_b, tokens_all, over_rows, preferred_element_type=jnp.float32
    )
    grad_out_part = lax.dot_general(
        combine_b, cotan_all, over_rows, preferred_element_type=jnp.float32
    )
    slot_sum = lax.psum(slot_part, "seq")
    slot_in = slot_sum.astype(jnp.bfloat16)
    pre = jnp.einsum("sd,sdf->sf", slot_in, expert_in, preferred_element_type=jnp.float32)
    hidden = gelu_tanh(pre).astype(jnp.bfloat16)
    out_part = jnp.einsum("sf,sfd->sd", hidden, expert_out, preferred_element_type=jnp.float32)
    slot_out = lax.psum(out_part, "seq").astype(jnp.bfloat16)
    grad_out_sum = lax.psum(grad_out_part, "seq")
    grad_slot_out = grad_out_sum.astype(jnp.bfloat16)
    out_grad = jnp.einsum(
        "sf,sd->sfd", hidden, grad_slot_out, preferred_element_type=jnp.float32
    ).astype(jnp.bfloat16)
    grad_hidden = jnp.einsum(
        "sd,sfd->sf", grad_slot_out, expert_out, preferred_element_type=jnp.float32
    )
    unused, back = jax.vjp(gelu_tanh, pre)
    grad_pre = back(grad_hidden)[0].astype(jnp.bfloat16)
    in_grad = jnp.einsum(
        "sd,sf->sdf", slot_in, grad_pre, preferred_element_type=jnp.float32
    ).astype(jnp.bfloat16)
    grad_in_part = jnp.einsum("sf,sdf->sd", grad_pre, expert_in, preferred_element_type=jnp.float32)
    grad_slot_in = lax.psum(grad_in_part, "seq").astype(jnp.bfloat16)
    grad_combine = lax.dot_general(
        cotan_all, slot_out, over_cols, preferred_element_type=jnp.float32
    )
    combine_row = lax.psum(jnp.sum(combine * grad_combine, axis=1), "exp")
    logit_comb = combine * (grad_combine - combine_row[:, None])
    grad_dispatch = lax.dot_general(
        tokens_all, grad_slot_in, over_cols, preferred_element_type=jnp.float32
    )
    grad_logits = (column_back(dispatch, grad_dispatch) + logit_comb).astype(jnp.bfloat16)
    key_part = lax.dot_general(
        tokens_all, grad_logits, over_rows, preferred_element_type=jnp.float32
    )
    key_grad = key_total(key_part)
    token_part = jnp.dot(dispatch_b, grad_slot_in, preferred_element_type=jnp.float32)
    token_part = token_part + lax.dot_general(
        grad_logits, slot_keys, over_cols, preferred_element_type=jnp.float32
    )
    token_grad = lax.psum_scatter(token_part, "exp", scatter_dimension=1, tiled=True).astype(
        jnp.bfloat16
    )
    return (token_grad, key_grad, in_grad, out_grad)


def solution(mesh):
    return jax.shard_map(
        per_device,
        mesh=mesh,
        in_specs=(
            P("seq", "exp"),
            P("seq", "exp"),
            P(None, "exp"),
            P("exp", None, "seq"),
            P("exp", "seq", None),
        ),
        out_specs=(P("seq", "exp"), P("seq", "exp"), P("exp", None, "seq"), P("exp", "seq", None)),
        check_vma=False,
    )
```

profile of v0, /device:TPU:1, one launch (start us, length us, event | category | flops | bytes accessed | tf_op | source)
XLA Modules:
  0.0 1290.7 jit_solution(5019178521883885787)
XLA Ops:
  7.2 0.0 copy-start
  7.2 0.0 all-gather.7.cloned.1.call-start
  7.2 0.7 all-gather.7.cloned.1.call-update
  7.9 0.0 all-gather.9.cloned.1.call-start
  8.0 0.7 all-gather.9.cloned.1.call-update
  8.7 0.0 reduce-scatter.7.cloned.1.call-start
  8.7 0.0 copy-start.3
  8.7 67.5 %all-gather.7.cloned.1.call-done = bf16[256,2048]{1,0:T(8,128)(2,1)} async-done(((bf16[256,256]{1,0:T(8,128)(2,1)}), bf16[256,2048]{1,0:T(8,128)(2,1)}) %all-gather.7.cloned.1.call-update) | async-done | bytes 1048592 | tf_op jit(solution)/shard_map/all_gather | solution.py:45
  76.2 1.7 fusion.26
  77.9 106.0 %pmax.7 = f32[2]{0:T(128)S(1)} all-reduce(f32[2]{0:T(128)S(1)} %get-tuple-element.37), channel_id=1, replica_groups=mesh['seq'=64,'exp'=8] {'seq'}, use_global_device_ids=true, to_apply=%region_1.0 | all-reduce | flops 2 | bytes 16 | tf_op jit(solution)/shard_map/pmax | solution.py:26
  183.9 0.2 exponential_reduce_fusion
  184.1 17.1 %all-gather.3 = f32[8,1,256]{2,1,0:T(1,128)S(1)} all-gather(f32[1,1,256]{2,1,0:T(1,128)S(1)} %bitcast.71), channel_id=3, replica_groups=mesh['seq'=64,'exp'=8] {'exp'}, dimensions={0}, use_global_device_ids=true | all-gather | bytes 9216 | tf_op jit(solution)/shard_map/all_gather | solution.py:8
  201.2 14.6 %all-gather.2 = f32[8,1,256]{2,1,0:T(1,128)S(1)} all-gather(f32[1,1,256]{2,1,0:T(1,128)S(1)} %bitcast.66), channel_id=2, replica_groups=mesh['seq'=64,'exp'=8] {'exp'}, dimensions={0}, use_global_device_ids=true | all-gather | bytes 9216 | tf_op jit(solution)/shard_map/all_gather | solution.py:8
  215.9 114.0 %psum.49 = f32[2]{0:T(128)S(1)} all-reduce(f32[2]{0:T(128)S(1)} %get-tuple-element.35), channel_id=1, replica_groups=mesh['seq'=64,'exp'=8] {'seq'}, use_global_device_ids=true, to_apply=%region_3.0 | all-reduce | flops 2 | bytes 16 | tf_op jit(solution)/shard_map/psum | solution.py:28
  329.9 0.3 while.12
  330.2 0.1 exponential_divide_fusion
  330.3 1.5 fusion.24
  331.8 0.0 all-gather.9.cloned.1.call-done
  331.8 1.5 fusion.20
  333.2 203.6 %all-reduce.1 = (bf16[2,2048]{1,0:T(2,128)(2,1)S(1)}, bf16[2,2048]{1,0:T(2,128)(2,1)S(1)}) all-reduce(f32[2,2048]{1,0:T(2,128)S(1)} %fusion.24, f32[2,2048]{1,0:T(2,128)S(1)} %fusion.20), channel_id=1, replica_groups=mesh['seq'=64,'exp'=8] {'seq'}, use_global_device_ids=true, to_apply=%region_9.10 | all-reduce | flops 8192 | bytes 49152 | tf_op jit(solution)/shard_map/psum | solution.py:63
  536.8 0.0 copy-done
  536.8 0.2 fusion
  537.1 0.0 copy-done.3
  537.1 0.4 fusion.2
  537.5 0.0 copy-start.1
  537.5 0.4 fusion.18
  537.9 207.4 %psum.52 = bf16[2,2048]{1,0:T(2,128)(2,1)S(1)} all-reduce(f32[2,2048]{1,0:T(2,128)S(1)} %bitcast.61), channel_id=1, replica_groups=mesh['seq'=64,'exp'=8] {'seq'}, use_global_device_ids=true, to_apply=%region_10.11 | all-reduce | flops 4096 | bytes 24576 | tf_op jit(solution)/shard_map/psum | solution.py:83
  745.3 1.8 fusion.6
  747.2 0.2 fusion.16
  747.4 0.0 copy-done.1
  747.4 0.5 multiply_reduce_fusion.1
  747.9 207.4 %all-reduce = (bf16[2,2048]{1,0:T(2,128)(2,1)S(1)}, f32[2]{0:T(128)S(1)}) all-reduce(f32[2,2048]{1,0:T(2,128)S(1)} %bitcast.60, f32[2]{0:T(128)S(1)} %get-tuple-element.65), channel_id=1, replica_groups=mesh['seq'=64,'exp'=8] {'seq'}, use_global_device_ids=true, to_apply=%region_13.14 | all-reduce | flops 4098 | bytes 24592 | tf_op jit(solution)/shard_map/psum | solution.py:68
  955.3 0.0 copy-start.4
  955.3 1.6 multiply_reduce_fusion
  957.0 17.2 %psum.55 = f32[256]{0:T(256)S(1)} all-reduce(f32[256]{0:T(256)S(1)} %get-tuple-element.67), channel_id=1, replica_groups=mesh['seq'=64,'exp'=8] {'exp'}, use_global_device_ids=true, to_apply=%region_15.16 | all-reduce | flops 256 | bytes 2048 | tf_op jit(solution)/shard_map/psum | solution.py:87
  974.2 0.3 convolution_bitcast_fusion
  974.5 0.0 copy-start.2
  974.5 1.4 copy.17
  975.9 0.0 reduce-scatter.7.cloned.1.call-update
  975.9 0.0 reduce-scatter.5.cloned.1.call-start
  975.9 0.0 copy-done.4
  975.9 0.5 copy-done.2
  976.5 1.9 convolution_add_fusion
  978.4 0.0 reduce-scatter.5.cloned.1.call-update
  978.4 1.1 multiply_convert_fusion
  979.6 1.6 multiply_convert_fusion.1
  981.1 212.7 %reduce-scatter.7.cloned.1.call-done = f32[32,2]{1,0:T(8,128)} async-done(((f32[2048,2]{1,0:T(8,128)}), f32[32,2]{1,0:T(8,128)}) %reduce-scatter.7.cloned.1.call-update) | async-done | bytes 272
  1193.8 1.4 copy.18
  1195.2 87.4 %reduce-scatter.5.cloned.1.call-done = f32[256,256]{1,0:T(8,128)} async-done(((f32[256,2048]{1,0:T(8,128)}), f32[256,256]{1,0:T(8,128)}) %reduce-scatter.5.cloned.1.call-update) | async-done | bytes 262160 | tf_op jit(solution)/shard_map/reduce_scatter | solution.py:101
  1282.6 1.6 convert_element_type.45
  (25 shorter events, 0.3 us)
Async XLA Ops:
  7.2 529.7 %copy-start = (bf16[2,2048,128]{2,1,0:T(8,128)(2,1)S(1)}, bf16[2,2048,128]{2,1,0:T(8,128)(2,1)}, u32[]{:S(2)}) copy-start(bf16[2,2048,128]{2,1,0:T(8,128)(2,1)} %param.10) | copy-start | bytes 3145732
  7.2 69.0 %all-gather.7.cloned.1.call-start = ((), (), s32[]{:S(2)}) async-start(), calls=%async_computation.2 | async-start | bytes 1179648 | tf_op jit(solution)/shard_map/all_gather | solution.py:45
  7.9 323.8 %all-gather.9.cloned.1.call-start = ((), (), s32[]{:S(2)}) async-start(), calls=%async_computation.3 | async-start | bytes 1179648 | tf_op jit(solution)/shard_map/all_gather | solution.py:46
  8.7 1185.2 %reduce-scatter.7.cloned.1.call-start = ((), (), s32[]{:S(2)}) async-start(), calls=%async_computation.5 | async-start | bytes 1064960
  8.7 528.4 %copy-start.3 = (bf16[2,128,2048]{2,1,0:T(8,128)(2,1)S(1)}, bf16[2,128,2048]{2,1,0:T(8,128)(2,1)}, u32[]{:S(2)}) copy-start(bf16[2,128,2048]{2,1,0:T(8,128)(2,1)} %param.11) | copy-start | bytes 3145732
  537.5 209.9 %copy-start.1 = (bf16[256,2048]{1,0:T(8,128)(2,1)S(1)}, bf16[256,2048]{1,0:T(8,128)(2,1)}, u32[]{:S(2)}) copy-start(bf16[256,2048]{1,0:T(8,128)(2,1)} %all-gather.7.cloned.1.call-done) | copy-start | bytes 3145732
  955.3 20.6 %copy-start.4 = (bf16[2048,2]{0,1:T(2,128)(2,1)S(1)}, bf16[2048,2]{0,1:T(2,128)(2,1)}, u32[]{:S(2)}) copy-start(bf16[2048,2]{0,1:T(2,128)(2,1)} %param.9) | copy-start | bytes 24580
  974.5 2.0 copy-start.2
  975.9 306.7 %reduce-scatter.5.cloned.1.call-start = ((), (), s32[]{:S(2)}) async-start(), calls=%async_computation.4 | async-start | bytes 2359296 | tf_op jit(solution)/shard_map/reduce_scatter | solution.py:101
Sparse Core Ops, SparseCore 0:
  11.1 65.0 all-gather.6
  79.2 59.0 all-gather.8
  976.0 217.7 reduce-scatter.6
  1198.9 83.6 reduce-scatter.4
where the time goes:
time: 1290 us
  blocking collectives  887 us (69%)
  waiting for transfers between devices  369 us (29%)
  between operations  13.9 us (1%)
    unnamed x5, waiting for transfers between devices  214 us
    psum x1, blocking collectives, per_device(): slot_out = lax.psum(out_part, 'seq').astype(jnp.bfloat16)  207 us
    psum x1, blocking collectives, per_device(): grad_slot_in = lax.psum(grad_in_part, 'seq').astype(jnp.bfloat16)  207 us
    psum x1, blocking collectives, per_device(): slot_sum = lax.psum(slot_part, 'seq')  204 us
    psum x1, blocking collectives, column_stats(): col_total = lax.psum(jnp.sum(col_exp, axis=0), 'seq')  114 us
    pmax x1, blocking collectives, column_stats(): col_peak = lax.pmax(jnp.max(logits, axis=0), 'seq')  106 us
    reduce_scatter x1, waiting for transfers between devices, per_device(): lax.psum_scatter(token_part, 'exp', scatter_dimension=1, tiled=True)  87.4 us
    all_gather x1, waiting for transfers between devices, per_device(): lax.all_gather(tokens, 'exp', axis=1, tiled=True)  67.5 us
  transfers between devices with their start and end apart: 4, of which 3 were waited for; matrix products, arithmetic and copies ran while one was open for 1% of the time, Pallas kernels for 0%

commit v1 on v0

v1 whole, which is shorter than its diff:
```python
import jax
import jax.numpy as jnp
from jax import lax
from jax.experimental import pallas as pl
from jax.experimental.pallas import tpu as pltpu
from jax.sharding import PartitionSpec as P

MESH = pl.DeviceIdType.MESH
F32, BF16 = jnp.float32, jnp.bfloat16
ROOT_2_PI, CUBE = 0.7978845608, 0.044715


def dot(lhs, rhs, lhs_dim, rhs_dim):
    return lax.dot_general(
        lhs, rhs, (((lhs_dim,), (rhs_dim,)), ((), ())), preferred_element_type=F32
    )


def kernel(
    keys_ref, tokens_hbm, cotan_hbm, win_hbm, wout_hbm,
    token_grad_ref, key_row_ref, in_grad_hbm, out_grad_hbm,
    tok, cot, win, wout, in_grad, out_grad,
    key_buf, log_src, log_buf, c1_src, c1_buf, z_src, z_buf, d_buf,
    e1_src, e1_buf, e2_src, e2_buf, e3_src, e3_buf, g_src, g_buf, h_src, h_buf,
    gsi_rows, lse_rows, load_sem, store_sem, send_sem, recv_sem,
):
    i, e = lax.axis_index("seq"), lax.axis_index("exp")
    x_lo, z, core = i // 32, (i // 2) % 16, i % 2
    q = x_lo * 2 + core

    def seq_of(quarter, z_at):
        return (quarter // 2) * 32 + z_at * 2 + quarter % 2

    loads = [
        pltpu.make_async_copy(src, dst, load_sem.at[n])
        for n, (src, dst) in enumerate(
            ((tokens_hbm, tok), (cotan_hbm, cot), (win_hbm, win), (wout_hbm, wout))
        )
    ]
    for load in loads:
        load.start()

    barrier = pltpu.get_barrier_semaphore()
    for k in range(1, 8):
        pl.semaphore_signal(barrier, 1, device_id=(i, (e + k) % 8), device_id_type=MESH)
    for k in range(1, 64):
        pl.semaphore_signal(barrier, 1, device_id=((i + k) % 64, e), device_id_type=MESH)
    pl.semaphore_wait(barrier, 70)

    def send(phase, src, dst, seq_at, exp_at):
        pltpu.make_async_remote_copy(
            src, dst, send_sem.at[phase], recv_sem.at[phase],
            device_id=(seq_at, exp_at), device_id_type=MESH,
        ).start()

    def keep(phase, src, dst):
        pltpu.make_async_copy(src, dst, recv_sem.at[phase]).start()

    def arrive(phase, ref):
        pltpu.make_async_copy(ref, ref, recv_sem.at[phase]).wait()

    def sent(phase, ref):
        pltpu.make_async_copy(ref, ref, send_sem.at[phase]).wait()

    for k in range(1, 8):
        to = (e + k) % 8
        send(0, keys_ref.at[to], key_buf.at[e], i, to)
    key_buf[e] = keys_ref[e]
    loads[0].wait()
    arrive(0, key_buf.at[pl.ds(0, 7)])
    keys = key_buf[...].reshape(16, 256).astype(BF16)

    log_src[...] = dot(keys, tok[...], 1, 1)
    for k in range(1, 8):
        to = (e + k) % 8
        send(1, log_src, log_buf.at[e], i, to)
    log_buf[e] = log_src[...]
    loads[1].wait()
    arrive(1, log_buf.at[pl.ds(0, 7)])
    logits = log_buf[0]
    for k in range(1, 8):
        logits = logits + log_buf[k]

    peak = jnp.max(logits, axis=1, keepdims=True)
    weight_b = jnp.exp(logits - peak).astype(BF16)
    weight = weight_b.astype(F32)
    total = jnp.sum(weight, axis=1, keepdims=True)
    lse = peak + jnp.log(total)
    row_exp = jnp.exp(logits - jnp.max(logits, axis=0, keepdims=True))
    combine = row_exp / jnp.sum(row_exp, axis=0, keepdims=True)

    slot_part = dot(weight_b, tok[...], 1, 0) / total
    gout_part = dot(combine.astype(BF16), cot[...], 1, 0) * 16.0
    lse_wide = jnp.broadcast_to(lse, (16, 256))
    for b in range(8):
        c1_src[b, 0:2] = slot_part[2 * b : 2 * b + 2]
        c1_src[b, 2:4] = gout_part[2 * b : 2 * b + 2]
        c1_src[b, 4:6] = lse_wide[2 * b : 2 * b + 2]
        c1_src[b, 6:8] = jnp.zeros((2, 256), F32)
    home = seq_of(e // 2, z)
    c1_self = home == i
    for k in range(8):
        to = (e + k) % 8
        if k == 0:
            @pl.when(c1_self)
            def _():
                keep(2, c1_src.at[to], c1_buf.at[e % 2, q])

            @pl.when(jnp.logical_not(c1_self))
            def _():
                send(2, c1_src.at[to], c1_buf.at[e % 2, q], home, to)
        else:
            send(2, c1_src.at[to], c1_buf.at[e % 2, q], home, to)
    arrive(2, c1_buf)
    for h in range(2):
        part = [c1_buf[h, n] for n in range(4)]
        top = part[0][4:6]
        for n in range(1, 4):
            top = jnp.maximum(top, part[n][4:6])
        scale = [jnp.exp(part[n][4:6] - top) for n in range(4)]
        norm = scale[0] + scale[1] + scale[2] + scale[3]
        acc = part[0][0:2] * scale[0]
        gout = part[0][2:4]
        for n in range(1, 4):
            acc = acc + part[n][0:2] * scale[n]
            gout = gout + part[n][2:4]
        z_src[4 * h : 4 * h + 2, 0:256] = acc / norm
        z_src[4 * h + 2 : 4 * h + 4, 0:256] = gout
        z_src[4 * h : 4 * h + 2, 256:384] = (top + jnp.log(norm))[:, 0:128]
        z_src[4 * h + 2 : 4 * h + 4, 256:384] = jnp.zeros((2, 128), F32)

    for k in range(1, 16):
        send(3, z_src, z_buf.at[z], seq_of(q, (z + k) % 16), e)
    z_buf[z] = z_src[...]
    arrive(3, z_buf.at[pl.ds(0, 15)])
    top = z_buf[0, :, 256:384]
    for n in range(1, 16):
        top = jnp.maximum(top, z_buf[n, :, 256:384])
    norm = jnp.zeros((8, 128), F32)
    low, high = jnp.zeros((8, 128), F32), jnp.zeros((8, 128), F32)
    for n in range(16):
        scale = jnp.exp(z_buf[n, :, 256:384] - top)
        norm = norm + scale
        low = low + scale * z_buf[n, :, 0:128]
        high = high + scale * z_buf[n, :, 128:256]
    chunk = jnp.concatenate([low / norm, high / norm], axis=1)
    lse_all = top + jnp.log(norm)

    d_buf[q] = chunk
    for k in range(1, 4):
        send(4, d_buf.at[q], d_buf.at[q], seq_of((q + k) % 4, z), e)
    loads[2].wait()
    loads[3].wait()
    arrive(4, d_buf.at[pl.ds(0, 3)])

    vec = [d_buf[n].astype(BF16) for n in range(4)]
    pre, grad_hidden = [], []
    for s in range(2):
        total_p, total_g = [None, None], [None, None]
        for n in range(4):
            for h in range(2):
                at = n * 512 + h * 256
                p = dot(vec[n], win[s, at : at + 256, :], 1, 0)
                g = dot(vec[n], wout[s, :, at : at + 256], 1, 1)
                total_p[h] = p if total_p[h] is None else total_p[h] + p
                total_g[h] = g if total_g[h] is None else total_g[h] + g
        pre.append(total_p[0][s : s + 1] + total_p[1][4 + s : 5 + s])
        grad_hidden.append(total_g[0][2 + s : 3 + s] + total_g[1][6 + s : 7 + s])
    pre = jnp.concatenate(pre, axis=0)
    grad_hidden = jnp.concatenate(grad_hidden, axis=0)
    tanh = jnp.tanh(ROOT_2_PI * (pre + CUBE * pre * pre * pre))
    hidden = 0.5 * pre * (1.0 + tanh)
    slope = 0.5 * (1.0 + tanh) + 0.5 * pre * (1.0 - tanh * tanh) * ROOT_2_PI * (
        1.0 + 3.0 * CUBE * pre * pre
    )
    grad_pre = grad_hidden * slope
    zero = jnp.zeros((1, 128), F32)
    pad = jnp.zeros((6, 128), F32)
    hidden_b = [
        jnp.concatenate([hidden[0:1], zero, pad], axis=0).astype(BF16),
        jnp.concatenate([zero, hidden[1:2], pad], axis=0).astype(BF16),
    ]
    grad_pre_b = [
        jnp.concatenate([grad_pre[0:1], zero, pad], axis=0).astype(BF16),
        jnp.concatenate([zero, grad_pre[1:2], pad], axis=0).astype(BF16),
    ]

    for n in range(4):
        for h in range(2):
            at = n * 512 + h * 256
            out = dot(hidden_b[0], wout[0, :, at : at + 256], 1, 0) + dot(
                hidden_b[1], wout[1, :, at : at + 256], 1, 0
            )
            gin = dot(grad_pre_b[0], win[0, at : at + 256, :], 1, 1) + dot(
                grad_pre_b[1], win[1, at : at + 256, :], 1, 1
            )
            e1_src[n, 4 * h : 4 * h + 2, :] = gin[0:2]
            e1_src[n, 4 * h + 2 : 4 * h + 4, :] = out[0:2]
    for k in range(1, 4):
        to = (q + k) % 4
        send(5, e1_src.at[to], e1_buf.at[q], seq_of(to, z), e)
    e1_buf[q] = e1_src[q]
    arrive(5, e1_buf.at[pl.ds(0, 3)])
    e2_src[...] = (e1_buf[0] + e1_buf[1]) + (e1_buf[2] + e1_buf[3])
    for k in range(1, 16):
        send(6, e2_src, e2_buf.at[z], seq_of(q, (z + k) % 16), e)
    e2_buf[z] = e2_src[...]

    for s in range(2):
        for n in range(4):
            for h in range(2):
                at = n * 512 + h * 256
                mask_in = lax.broadcasted_iota(jnp.int32, (8, 128), 0) == 4 * h + s
                rows_in = jnp.where(mask_in, grad_pre[s : s + 1], 0.0).astype(BF16)
                in_grad[s, at : at + 256, :] = dot(vec[n], rows_in, 0, 0).astype(BF16)
                mask_out = lax.broadcasted_iota(jnp.int32, (8, 128), 0) == 4 * h + 2 + s
                rows_out = jnp.where(mask_out, hidden[s : s + 1], 0.0).astype(BF16)
                out_grad[s, :, at : at + 256] = dot(rows_out, vec[n], 0, 0).astype(BF16)
    stores = [
        pltpu.make_async_copy(in_grad, in_grad_hbm, store_sem.at[0]),
        pltpu.make_async_copy(out_grad, out_grad_hbm, store_sem.at[1]),
    ]
    for store in stores:
        store.start()

    arrive(6, e2_buf.at[pl.ds(0, 15)])
    full = e2_buf[0]
    for n in range(1, 16):
        full = full + e2_buf[n]
    full = full.astype(BF16).astype(F32)
    inner = jnp.sum(full * chunk, axis=1, keepdims=True)
    inner = jnp.broadcast_to(inner, (8, 256))
    lse_pair = jnp.concatenate([lse_all, lse_all], axis=1)
    for h in range(2):
        e3_src[h, 0:4] = full[4 * h : 4 * h + 4]
        e3_src[h, 4:6] = lse_pair[0:2]
        e3_src[h, 6:8] = inner[4 * h : 4 * h + 2]

    for k in range(4):
        to_q = (q + k) % 4
        for h in range(2):
            to_e = 2 * q + h
            if k == 0:
                @pl.when(to_e == e)
                def _():
                    keep(7, e3_src.at[h], e3_buf.at[e])

                @pl.when(to_e != e)
                def _():
                    send(7, e3_src.at[h], e3_buf.at[e], seq_of(to_q, z), to_e)
            else:
                send(7, e3_src.at[h], e3_buf.at[e], seq_of(to_q, z), to_e)
    arrive(7, e3_buf)
    stack = e3_buf[...].reshape(64, 256).astype(BF16)
    by_cot = dot(stack, cot[...], 1, 1)
    by_tok = dot(stack, tok[...], 1, 1)
    for b in range(8):
        g_src[2 * b : 2 * b + 2] = by_tok[8 * b : 8 * b + 2] - e3_buf[b, 6:8]
        g_src[16 + 2 * b : 18 + 2 * b] = by_cot[8 * b + 2 : 8 * b + 4]
    for k in range(1, 8):
        to = (e + k) % 8
        send(8, g_src, g_buf.at[e], i, to)
    g_buf[e] = g_src[...]
    for b in range(8):
        gsi_rows[2 * b : 2 * b + 2] = e3_buf[b, 0:2]
        lse_rows[2 * b : 2 * b + 2] = e3_buf[b, 4:6]
    dispatch = weight * (jnp.exp(lse - lse_rows[...]) / total)
    arrive(8, g_buf.at[pl.ds(0, 7)])
    grads = g_buf[0]
    for k in range(1, 8):
        grads = grads + g_buf[k]
    grad_dispatch, grad_combine = grads[0:16], grads[16:32]
    combine_row = jnp.sum(combine * grad_combine, axis=0, keepdims=True)
    grad_logits = dispatch * grad_dispatch + combine * (grad_combine - combine_row)
    grad_logits_b = grad_logits.astype(BF16)

    key_part = dot(grad_logits_b, tok[...], 1, 0)
    lane = lax.broadcasted_iota(jnp.int32, (16, 128), 1)
    for a in range(8):
        own = (key_part if a == 0 else pltpu.roll(key_part, 256 - 32 * a, 1))[:, 0:128]
        odd = pltpu.roll(pltpu.roll(own, 32, 1), 15, 0)
        row = jnp.where(lane < 32, own, odd)
        for b in range(8):
            h_src[a * 8 + b] = row[2 * b : 2 * b + 1]
    h_here = i // 8 == e

    for k in range(8):
        for m in range(8):
            a, b = (i + k) % 8, (e + m) % 8
            to = 8 * e + a
            if k == 0 and m == 0:
                @pl.when(h_here)
                def _():
                    keep(9, h_src.at[a * 8 + b], h_buf.at[i])

                @pl.when(jnp.logical_not(h_here))
                def _():
                    send(9, h_src.at[a * 8 + b], h_buf.at[i], to, b)
            else:
                send(9, h_src.at[a * 8 + b], h_buf.at[i], to, b)

    left = jnp.concatenate([dispatch.astype(BF16), grad_logits_b], axis=0)
    right = jnp.concatenate([gsi_rows[...].astype(BF16), keys], axis=0)
    token_grad_ref[...] = dot(left, right, 0, 0).astype(BF16)
    arrive(9, h_buf)
    rows = h_buf[0]
    for n in range(1, 64):
        rows = rows + h_buf[n]
    key_row_ref[...] = rows

    for store in stores:
        store.wait()
    sent(0, key_buf.at[pl.ds(0, 7)])
    sent(1, log_buf.at[pl.ds(0, 7)])

    @pl.when(c1_self)
    def _():
        sent(2, c1_src.at[pl.ds(0, 7)])

    @pl.when(jnp.logical_not(c1_self))
    def _():
        sent(2, c1_src)

    sent(3, z_buf.at[pl.ds(0, 15)])
    sent(4, d_buf.at[pl.ds(0, 3)])
    sent(5, e1_buf.at[pl.ds(0, 3)])
    sent(6, e2_buf.at[pl.ds(0, 15)])

    @pl.when(e // 2 == q)
    def _():
        sent(7, e3_buf.at[pl.ds(0, 7)])

    @pl.when(e // 2 != q)
    def _():
        sent(7, e3_buf)

    sent(8, g_buf.at[pl.ds(0, 7)])

    @pl.when(h_here)
    def _():
        sent(9, h_buf.at[pl.ds(0, 63)])

    @pl.when(jnp.logical_not(h_here))
    def _():
        sent(9, h_buf)


def per_device(tokens, cotangent, slot_keys, expert_in, expert_out):
    keys = slot_keys.astype(F32).T.reshape(2, 8, 256).transpose(1, 0, 2)
    any_space = pl.BlockSpec(memory_space=pl.ANY)
    vmem = pl.BlockSpec(memory_space=pltpu.VMEM)
    buf = pltpu.VMEM
    token_grad, key_row, in_grad, out_grad = pl.pallas_call(
        kernel,
        out_shape=(
            jax.ShapeDtypeStruct((256, 256), BF16),
            jax.ShapeDtypeStruct((1, 128), F32),
            jax.ShapeDtypeStruct((2, 2048, 128), BF16),
            jax.ShapeDtypeStruct((2, 128, 2048), BF16),
        ),
        in_specs=[vmem, any_space, any_space, any_space, any_space],
        out_specs=(vmem, vmem, any_space, any_space),
        scratch_shapes=[
            buf((256, 256), BF16), buf((256, 256), BF16),
            buf((2, 2048, 128), BF16), buf((2, 128, 2048), BF16),
            buf((2, 2048, 128), BF16), buf((2, 128, 2048), BF16),
            buf((8, 2, 256), F32),
            buf((16, 256), F32), buf((8, 16, 256), F32),
            buf((8, 8, 256), F32), buf((2, 4, 8, 256), F32),
            buf((8, 384), F32), buf((16, 8, 384), F32),
            buf((4, 8, 256), F32),
            buf((4, 8, 256), F32), buf((4, 8, 256), F32),
            buf((8, 256), F32), buf((16, 8, 256), F32),
            buf((2, 8, 256), F32), buf((8, 8, 256), F32),
            buf((32, 256), F32), buf((8, 32, 256), F32),
            buf((64, 1, 128), F32), buf((64, 1, 128), F32),
            buf((16, 256), F32), buf((16, 256), F32),
            pltpu.SemaphoreType.DMA((4,)), pltpu.SemaphoreType.DMA((2,)),
            pltpu.SemaphoreType.DMA((10,)), pltpu.SemaphoreType.DMA((10,)),
        ],
        compiler_params=pltpu.CompilerParams(
            collective_id=0, has_side_effects=True, vmem_limit_bytes=32 * 2**20
        ),
        name="soft_moe_backward",
    )(keys, tokens, cotangent, expert_in, expert_out)
    key_grad = key_row[0, :64].reshape(2, 32).T
    return (token_grad, key_grad, in_grad, out_grad)


def solution(mesh):
    return jax.shard_map(
        per_device,
        mesh=mesh,
        in_specs=(
            P("seq", "exp"),
            P("seq", "exp"),
            P(None, "exp"),
            P("exp", None, "seq"),
            P("exp", "seq", None),
        ),
        out_specs=(P("seq", "exp"), P("seq", "exp"), P("exp", None, "seq"), P("exp", "seq", None)),
        check_vma=False,
    )
```

time: 1290 us -> 88.8 us (0.07)
  blocking collectives: 887 us -> 0 us
  waiting for transfers between devices: 369 us -> 0 us
  Pallas kernels: 0 us -> 79.7 us
  between operations: 13.9 us -> 0.65 us
    psum x5 -> x0, blocking collectives: 750 us -> none  [the longest x1 207 us: per_device(): slot_out = lax.psum(out_part, 'seq').astype(jnp.bfloat16)]
    unnamed x5 -> x0, waiting for transfers between devices: 214 us -> none
    pmax x1 -> x0, blocking collectives: 106 us -> none  [column_stats(): col_peak = lax.pmax(jnp.max(logits, axis=0), 'seq')]
    reduce_scatter x1 -> x0, waiting for transfers between devices: 87.4 us -> none  [per_device(): lax.psum_scatter(token_part, 'exp', scatter_dimension=1, tiled=True)]
    pallas_call x0 -> x1, Pallas kernels: none -> 79.7 us  [per_device(): pl.pallas_call(kernel, out_shape=(jax.ShapeDtypeStruct((256, 256), BF16),...]
    all_gather x2 -> x0, waiting for transfers between devices: 67.5 us -> none  [the longest x1 67.5 us: per_device(): lax.all_gather(tokens, 'exp', axis=1, tiled=True)]
    all_gather x2 -> x0, blocking collectives: 31.8 us -> none  [combined_all(): pieces = jax.tree.map(lambda part: lax.all_gather(part, axis), value)]
  transfers between devices with their start and end apart: 4 -> 0, of which waited for: 3 -> 0; matrix products, arithmetic and copies ran while one was open for 1% -> 0% of each run, Pallas kernels for 0% -> 0%
where the time goes in v1:
time: 88.8 us; the launch traced here: 88.6 us
  Pallas kernels  79.7 us (90%)
  local copies, waits for them, and re-layouts  7.51 us (8%)
    pallas_call x1, Pallas kernels, per_device(): pl.pallas_call(kernel, out_shape=(jax.ShapeDtypeStruct((256, 256), BF16),...  79.7 us
    unnamed x11, local copies, waits for them, and re-layouts  6.85 us

profile of v1, /device:TPU:1, one launch (start us, length us, event | category | flops | bytes accessed | tf_op | source)
XLA Modules:
  0.0 88.6 jit_solution(1472395854029092447)
XLA Ops:
  0.6 0.7 transpose.22
  1.3 0.0 copy-start
  1.3 1.2 %copy-done = bf16[2,2048,128]{2,1,0:T(8,128)(2,1)S(1)} copy-done((bf16[2,2048,128]{2,1,0:T(8,128)(2,1)S(1)}, bf16[2,2048,128]{2,1,0:T(8,128)(2,1)}, u32[]{:S(2)}) %copy-start) | copy-done | bytes 1048600
  2.6 0.0 copy-start.1
  2.6 1.2 %copy-done.1 = bf16[2,128,2048]{2,1,0:T(8,128)(2,1)S(1)} copy-done((bf16[2,128,2048]{2,1,0:T(8,128)(2,1)S(1)}, bf16[2,128,2048]{2,1,0:T(8,128)(2,1)}, u32[]{:S(2)}) %copy-start.1) | copy-done | bytes 1048600
  3.8 0.0 copy-start.2
  3.8 0.9 %copy-done.2 = bf16[256,256]{1,0:T(8,128)(2,1)S(1)} copy-done((bf16[256,256]{1,0:T(8,128)(2,1)S(1)}, bf16[256,256]{1,0:T(8,128)(2,1)}, u32[]{:S(2)}) %copy-start.2) | copy-done | bytes 131096
  4.7 0.0 copy-start.3
  4.7 0.9 %copy-done.3 = bf16[256,256]{1,0:T(8,128)(2,1)S(1)} copy-done((bf16[256,256]{1,0:T(8,128)(2,1)S(1)}, bf16[256,256]{1,0:T(8,128)(2,1)}, u32[]{:S(2)}) %copy-start.3) | copy-done | bytes 131096
  5.6 79.7 %soft_moe_backward.1 = (bf16[256,256]{1,0:T(8,128)(2,1)S(1)}, f32[1,128]{1,0:T(1,128)S(1)}, bf16[2,2048,128]{2,1,0:T(8,128)(2,1)S(1)}, bf16[2,128,2048]{2,1,0:T(8,128)(2,1)S(1)}) custom-call(f32[8,2,256]{2,1,0:T(2,128)S(1)} %bitcast.6, bf16[256,256]{1,0:T(8,128)(2,1)S(1)} %copy-done.2, bf16[256,256]{1,0:T(8,128)(2,1)S(1)} %copy-done.3, ...), custom_call_target="tpu_custom_call" | custom-call | tf_op jit(solution)/shard_map/soft_moe_backward/pallas_call | solution.py:353
  85.3 0.6 reshape_squeeze.3
  86.0 0.7 copy.12
  86.6 1.0 %copy.13 = bf16[2,2048,128]{2,1,0:T(8,128)(2,1)} copy(bf16[2,2048,128]{2,1,0:T(8,128)(2,1)S(1)} %get-tuple-element.18) | data formatting | bytes 2097152
  87.6 1.0 %copy.14 = bf16[2,128,2048]{2,1,0:T(8,128)(2,1)} copy(bf16[2,128,2048]{2,1,0:T(8,128)(2,1)S(1)} %get-tuple-element.19) | data formatting | bytes 2097152
  (1 shorter events, 0.0 us)
Async XLA Ops:
  1.3 1.2 %copy-start = (bf16[2,2048,128]{2,1,0:T(8,128)(2,1)S(1)}, bf16[2,2048,128]{2,1,0:T(8,128)(2,1)}, u32[]{:S(2)}) copy-start(bf16[2,2048,128]{2,1,0:T(8,128)(2,1)} %win_hbm.1) | copy-start | bytes 3145732
  2.6 1.2 %copy-start.1 = (bf16[2,128,2048]{2,1,0:T(8,128)(2,1)S(1)}, bf16[2,128,2048]{2,1,0:T(8,128)(2,1)}, u32[]{:S(2)}) copy-start(bf16[2,128,2048]{2,1,0:T(8,128)(2,1)} %wout_hbm.1) | copy-start | bytes 3145732
  3.8 0.9 %copy-start.2 = (bf16[256,256]{1,0:T(8,128)(2,1)S(1)}, bf16[256,256]{1,0:T(8,128)(2,1)}, u32[]{:S(2)}) copy-start(bf16[256,256]{1,0:T(8,128)(2,1)} %tokens_hbm.1) | copy-start | bytes 393220
  4.7 0.9 %copy-start.3 = (bf16[256,256]{1,0:T(8,128)(2,1)S(1)}, bf16[256,256]{1,0:T(8,128)(2,1)}, u32[]{:S(2)}) copy-start(bf16[256,256]{1,0:T(8,128)(2,1)} %cotan_hbm.1) | copy-start | bytes 393220

commit v2 on v1

v2 whole, which is shorter than its diff:
```python
import jax
import jax.numpy as jnp
from jax import lax
from jax.experimental import pallas as pl
from jax.experimental.pallas import tpu as pltpu
from jax.sharding import PartitionSpec as P

MESH = pl.DeviceIdType.MESH
F32, BF16 = jnp.float32, jnp.bfloat16
ROOT_2_PI, CUBE = 0.7978845608, 0.044715


def dot(lhs, rhs, lhs_dim, rhs_dim):
    return lax.dot_general(
        lhs, rhs, (((lhs_dim,), (rhs_dim,)), ((), ())), preferred_element_type=F32
    )


def kernel(
    keys_hbm, tokens_hbm, cotan_hbm, win_hbm, wout_hbm,
    token_grad_ref, key_ref, in_grad, out_grad,
    key_raw, tok, cot, win, wout,
    key_src, key_buf, log_src, log_buf, c1_src, c1_buf, z_src, z_buf, d_buf,
    e1_src, e1_buf, e2_src, e2_buf, e3_src, e3_buf, g_src, g_buf, h_src, h_buf,
    gsi_rows, lse_rows, load_sem, meet_sem, send_sem, recv_sem,
):
    i, e = lax.axis_index("seq"), lax.axis_index("exp")
    x_lo, z, core = i // 32, (i // 2) % 16, i % 2
    pair, own = z // 2, 2 * (x_lo * 2 + core) + z % 2

    def seq_of(member, pair_at):
        return (member // 4) * 32 + (pair_at * 2 + member % 2) * 2 + (member // 2) % 2

    loads = [
        pltpu.make_async_copy(src, dst, load_sem.at[n])
        for n, (src, dst) in enumerate(
            ((keys_hbm, key_raw), (tokens_hbm, tok), (cotan_hbm, cot), (win_hbm, win), (wout_hbm, wout))
        )
    ]
    for load in loads:
        load.start()

    def signal(sem, seq_at, exp_at):
        pl.semaphore_signal(sem, 1, device_id=(seq_at, exp_at), device_id_type=MESH)

    def meet(step):
        signal(meet_sem.at[step], seq_of(own, (pair + 2**step) % 8), e)
        signal(meet_sem.at[step], seq_of(own, (pair + 8 - 2**step) % 8), e)

    def met(step):
        pl.semaphore_wait(meet_sem.at[step], 2)

    barrier = pltpu.get_barrier_semaphore()
    for k in range(1, 8):
        signal(barrier, i, (e + k) % 8)
    for k in range(1, 8):
        signal(barrier, seq_of((own + k) % 8, pair), e)
    for k in (1, 7):
        signal(barrier, seq_of(own, (pair + k) % 8), e)
    loads[0].wait()
    keys_wide = key_raw[...].astype(F32)
    for k in range(8):
        key_src[k] = keys_wide[:, 256 * k : 256 * k + 256]
    pl.semaphore_wait(barrier, 16)

    def send(phase, src, dst, seq_at, exp_at):
        pltpu.make_async_remote_copy(
            src, dst, send_sem.at[phase], recv_sem.at[phase],
            device_id=(seq_at, exp_at), device_id_type=MESH,
        ).start()

    def send_or_keep(phase, here, src, dst, seq_at, exp_at):
        @pl.when(here)
        def _():
            pltpu.make_async_copy(src, dst, recv_sem.at[phase]).start()

        @pl.when(jnp.logical_not(here))
        def _():
            send(phase, src, dst, seq_at, exp_at)

    def arrive(phase, ref):
        pltpu.make_async_copy(ref, ref, recv_sem.at[phase]).wait()

    def sent(phase, ref):
        pltpu.make_async_copy(ref, ref, send_sem.at[phase]).wait()

    def sent_some(phase, here, ref, count):
        @pl.when(here)
        def _():
            sent(phase, ref.at[pl.ds(0, count - 1)])

        @pl.when(jnp.logical_not(here))
        def _():
            sent(phase, ref)

    for k in range(1, 8):
        to = (e + k) % 8
        send(0, key_src.at[to], key_buf.at[e], i, to)
    meet(0)
    key_buf[e] = key_src[e]
    loads[1].wait()
    arrive(0, key_buf.at[pl.ds(0, 7)])
    keys = key_buf[...].reshape(16, 256).astype(BF16)

    log_src[...] = dot(keys, tok[...], 1, 1)
    for k in range(1, 8):
        to = (e + k) % 8
        send(1, log_src, log_buf.at[e], i, to)
    met(0)
    meet(1)
    log_buf[e] = log_src[...]
    loads[2].wait()
    arrive(1, log_buf.at[pl.ds(0, 7)])
    logits = log_buf[0]
    for k in range(1, 8):
        logits = logits + log_buf[k]

    peak = jnp.max(logits, axis=1, keepdims=True)
    weight_b = jnp.exp(logits - peak).astype(BF16)
    weight = weight_b.astype(F32)
    total = jnp.sum(weight, axis=1, keepdims=True)
    lse = peak + jnp.log(total)
    row_exp = jnp.exp(logits - jnp.max(logits, axis=0, keepdims=True))
    combine = row_exp / jnp.sum(row_exp, axis=0, keepdims=True)

    slot_part = dot(weight_b, tok[...], 1, 0) / total
    gout_part = dot(combine.astype(BF16), cot[...], 1, 0) * 8.0
    lse_wide = jnp.broadcast_to(lse, (16, 256))
    for b in range(8):
        c1_src[b, 0:2] = slot_part[2 * b : 2 * b + 2]
        c1_src[b, 2:4] = gout_part[2 * b : 2 * b + 2]
        c1_src[b, 4:6] = lse_wide[2 * b : 2 * b + 2]
        c1_src[b, 6:8] = jnp.zeros((2, 256), F32)
    home = seq_of(e, pair)
    c1_here = own == e
    send_or_keep(2, c1_here, c1_src.at[e], c1_buf.at[own], home, e)
    for k in range(1, 8):
        to = (e + k) % 8
        send(2, c1_src.at[to], c1_buf.at[own], home, to)
    met(1)
    arrive(2, c1_buf)
    part = [c1_buf[n] for n in range(8)]
    stat = [value[4:8] for value in part]
    top = stat[0]
    for n in range(1, 8):
        top = jnp.maximum(top, stat[n])
    norm, acc = jnp.zeros((4, 256), F32), jnp.zeros((4, 256), F32)
    for n in range(8):
        scale = jnp.exp(stat[n] - top)
        norm = norm + scale
        acc = acc + scale * part[n][0:4]
    row4 = lax.broadcasted_iota(jnp.int32, (4, 256), 0)
    first = row4 < 2
    z_src[:, 0:256] = jnp.where(first, acc / norm, acc)
    z_src[:, 256:384] = jnp.where(first, top + jnp.log(norm), 0.0)[:, 0:128]

    for k in range(1, 8):
        send(3, z_src, z_buf.at[pair], seq_of(own, (pair + k) % 8), e)
    z_buf[pair] = z_src[...]
    arrive(3, z_buf.at[pl.ds(0, 7)])
    top = z_buf[0, :, 256:384]
    for n in range(1, 8):
        top = jnp.maximum(top, z_buf[n, :, 256:384])
    norm = jnp.zeros((4, 128), F32)
    low, high = jnp.zeros((4, 128), F32), jnp.zeros((4, 128), F32)
    for n in range(8):
        scale = jnp.exp(z_buf[n, :, 256:384] - top)
        norm = norm + scale
        low = low + scale * z_buf[n, :, 0:128]
        high = high + scale * z_buf[n, :, 128:256]
    chunk = jnp.concatenate([low / norm, high / norm], axis=1)
    lse_all = top + jnp.log(norm)

    d_buf[own] = chunk
    for k in range(1, 8):
        send(4, d_buf.at[own], d_buf.at[own], seq_of((own + k) % 8, pair), e)
    loads[3].wait()
    loads[4].wait()
    arrive(4, d_buf.at[pl.ds(0, 7)])

    def win_at(n):
        at = n * 256
        return jnp.concatenate([win[0, at : at + 256, :], win[1, at : at + 256, :]], axis=1)

    def wout_at(n):
        return wout[:, :, n * 256 : n * 256 + 256].reshape(256, 256)

    vec = [d_buf[n].astype(BF16) for n in range(8)]
    pre = dot(vec[0], win_at(0), 1, 0)
    grad_hidden = dot(vec[0], wout_at(0), 1, 1)
    for n in range(1, 8):
        pre = pre + dot(vec[n], win_at(n), 1, 0)
        grad_hidden = grad_hidden + dot(vec[n], wout_at(n), 1, 1)
    pre, grad_hidden = pre[0:2], grad_hidden[2:4]
    tanh = jnp.tanh(ROOT_2_PI * (pre + CUBE * pre * pre * pre))
    hidden = 0.5 * pre * (1.0 + tanh)
    slope = 0.5 * (1.0 + tanh) + 0.5 * pre * (1.0 - tanh * tanh) * ROOT_2_PI * (
        1.0 + 3.0 * CUBE * pre * pre
    )
    lane4 = lax.broadcasted_iota(jnp.int32, (4, 256), 1)
    both = jnp.concatenate([grad_hidden * slope, hidden], axis=0)
    both = jnp.where((lane4 // 128) == (row4 % 2), both, 0.0)
    both_b = both.astype(BF16)

    for n in range(8):
        gin = dot(both_b, win_at(n), 1, 1)
        out = dot(both_b, wout_at(n), 1, 0)
        e1_src[n] = jnp.where(first, gin, out)
    for k in range(1, 8):
        to = (own + k) % 8
        send(5, e1_src.at[to], e1_buf.at[own], seq_of(to, pair), e)
    e1_buf[own] = e1_src[own]
    arrive(5, e1_buf.at[pl.ds(0, 7)])
    full = e1_buf[0]
    for n in range(1, 8):
        full = full + e1_buf[n]
    e2_src[...] = full
    for k in range(1, 8):
        send(6, e2_src, e2_buf.at[pair], seq_of(own, (pair + k) % 8), e)
    e2_buf[pair] = full

    pre_rows = jnp.where(first, both, 0.0).astype(BF16)
    hid_rows = jnp.where(first, 0.0, both).astype(BF16)
    for n in range(8):
        at = n * 256
        block = dot(vec[n], pre_rows, 0, 0).astype(BF16)
        in_grad[0, at : at + 256, :] = block[:, 0:128]
        in_grad[1, at : at + 256, :] = block[:, 128:256]
        block = dot(hid_rows, vec[n], 0, 0).astype(BF16)
        out_grad[:, :, at : at + 256] = block.reshape(2, 128, 256)

    arrive(6, e2_buf.at[pl.ds(0, 7)])
    full = e2_buf[0]
    for n in range(1, 8):
        full = full + e2_buf[n]
    full = full.astype(BF16).astype(F32)
    inner = jnp.sum(full * chunk, axis=1, keepdims=True)
    e3_src[0:4] = full
    e3_src[4:6] = jnp.concatenate([lse_all, lse_all], axis=1)[0:2]
    e3_src[6:8] = jnp.broadcast_to(inner, (4, 256))[0:2]

    send_or_keep(7, c1_here, e3_src, e3_buf.at[e], i, own)
    for k in range(1, 8):
        send(7, e3_src, e3_buf.at[e], seq_of((own + k) % 8, pair), own)
    arrive(7, e3_buf)
    stack = e3_buf[...].reshape(64, 256).astype(BF16)
    by_cot = dot(stack, cot[...], 1, 1)
    by_tok = dot(stack, tok[...], 1, 1)
    for b in range(8):
        g_src[2 * b : 2 * b + 2] = by_tok[8 * b : 8 * b + 2] - e3_buf[b, 6:8]
        g_src[16 + 2 * b : 18 + 2 * b] = by_cot[8 * b + 2 : 8 * b + 4]
    for k in range(1, 8):
        to = (e + k) % 8
        send(8, g_src, g_buf.at[e], i, to)
    g_buf[e] = g_src[...]
    for b in range(8):
        gsi_rows[2 * b : 2 * b + 2] = e3_buf[b, 0:2]
        lse_rows[2 * b : 2 * b + 2] = e3_buf[b, 4:6]
    dispatch = weight * (jnp.exp(lse - lse_rows[...]) / total)
    arrive(8, g_buf.at[pl.ds(0, 7)])
    grads = g_buf[0]
    for k in range(1, 8):
        grads = grads + g_buf[k]
    grad_dispatch, grad_combine = grads[0:16], grads[16:32]
    combine_row = jnp.sum(combine * grad_combine, axis=0, keepdims=True)
    grad_logits = dispatch * grad_dispatch + combine * (grad_combine - combine_row)
    grad_logits_b = grad_logits.astype(BF16)

    key_part = dot(grad_logits_b, tok[...], 1, 0)
    lane = lax.broadcasted_iota(jnp.int32, (16, 128), 1)
    for a in range(8):
        own = (key_part if a == 0 else pltpu.roll(key_part, 256 - 32 * a, 1))[:, 0:128]
        odd = pltpu.roll(pltpu.roll(own, 32, 1), 15, 0)
        row = jnp.where(lane < 32, own, odd)
        for b in range(8):
            h_src[a * 8 + b] = row[2 * b : 2 * b + 1]
    h_here = i // 8 == e
    for k in range(8):
        for m in range(8):
            a, b = (i + k) % 8, (e + m) % 8
            if k == 0 and m == 0:
                send_or_keep(9, h_here, h_src.at[a * 8 + b], h_buf.at[i], 8 * e + a, b)
            else:
                send(9, h_src.at[a * 8 + b], h_buf.at[i], 8 * e + a, b)

    left = jnp.concatenate([dispatch.astype(BF16), grad_logits_b], axis=0)
    right = jnp.concatenate([gsi_rows[...].astype(BF16), keys], axis=0)
    token_grad_ref[...] = dot(left, right, 0, 0).astype(BF16)
    arrive(9, h_buf)
    rows = h_buf[0]
    for n in range(1, 64):
        rows = rows + h_buf[n]
    key_ref[...] = jnp.concatenate([rows[:, 0:32], rows[:, 32:64]], axis=0)

    sent(0, key_buf.at[pl.ds(0, 7)])
    sent(1, log_buf.at[pl.ds(0, 7)])
    sent_some(2, c1_here, c1_src, 8)
    sent(3, z_buf.at[pl.ds(0, 7)])
    sent(4, d_buf.at[pl.ds(0, 7)])
    sent(5, e1_buf.at[pl.ds(0, 7)])
    sent(6, e2_buf.at[pl.ds(0, 7)])
    sent_some(7, c1_here, e3_buf, 8)
    sent(8, g_buf.at[pl.ds(0, 7)])
    sent_some(9, h_here, h_buf, 64)


def write_out(*refs):
    sems = refs[-1]
    count = (len(refs) - 1) // 2
    copies = [
        pltpu.make_async_copy(refs[n], refs[count + n], sems.at[n]) for n in range(count)
    ]
    for copy in copies:
        copy.start()
    for copy in copies:
        copy.wait()


def per_device(tokens, cotangent, slot_keys, expert_in, expert_out):
    any_space = pl.BlockSpec(memory_space=pl.ANY)
    buf = pltpu.VMEM
    outs = (
        ((256, 256), BF16), ((2, 32), F32), ((2, 2048, 128), BF16), ((2, 128, 2048), BF16)
    )
    big = [
        pltpu.with_memory_space_constraint(value, pltpu.HBM)
        for value in (slot_keys.T, tokens, cotangent, expert_in, expert_out)
    ]
    held = pl.pallas_call(
        kernel,
        out_shape=tuple(pltpu.VMEM(shape, kind) for shape, kind in outs),
        in_specs=[any_space] * 5,
        scratch_shapes=[
            buf((2, 2048), BF16), buf((256, 256), BF16), buf((256, 256), BF16),
            buf((2, 2048, 128), BF16), buf((2, 128, 2048), BF16),
            buf((8, 2, 256), F32), buf((8, 2, 256), F32),
            buf((16, 256), F32), buf((8, 16, 256), F32),
            buf((8, 8, 256), F32), buf((8, 8, 256), F32),
            buf((4, 384), F32), buf((8, 4, 384), F32),
            buf((8, 4, 256), F32),
            buf((8, 4, 256), F32), buf((8, 4, 256), F32),
            buf((4, 256), F32), buf((8, 4, 256), F32),
            buf((8, 256), F32), buf((8, 8, 256), F32),
            buf((32, 256), F32), buf((8, 32, 256), F32),
            buf((64, 1, 128), F32), buf((64, 1, 128), F32),
            buf((16, 256), F32), buf((16, 256), F32),
            pltpu.SemaphoreType.DMA((5,)),
            pltpu.SemaphoreType.REGULAR((2,)), pltpu.SemaphoreType.DMA((10,)), pltpu.SemaphoreType.DMA((10,)),
        ],
        compiler_params=pltpu.CompilerParams(
            collective_id=0, has_side_effects=True, vmem_limit_bytes=32 * 2**20
        ),
        name="soft_moe_backward",
    )(*big)
    token_grad, key_grad, in_grad, out_grad = pl.pallas_call(
        write_out,
        out_shape=tuple(pltpu.HBM(shape, kind) for shape, kind in outs),
        in_specs=[any_space] * 4,
        out_specs=(any_space,) * 4,
        scratch_shapes=[pltpu.SemaphoreType.DMA((4,))],
        compiler_params=pltpu.CompilerParams(vmem_limit_bytes=2**20),
        name="write_out",
    )(*held)
    return (token_grad, key_grad.T, in_grad, out_grad)


def solution(mesh):
    return jax.shard_map(
        per_device,
        mesh=mesh,
        in_specs=(
            P("seq", "exp"),
            P("seq", "exp"),
            P(None, "exp"),
            P("exp", None, "seq"),
            P("exp", "seq", None),
        ),
        out_specs=(P("seq", "exp"), P("seq", "exp"), P("exp", None, "seq"), P("exp", "seq", None)),
        check_vma=False,
    )
```

time: 88.8 us -> 72.2 us (0.81)
  Pallas kernels: 79.7 us -> 71.5 us
  local copies, waits for them, and re-layouts: 7.51 us -> 0 us
    pallas_call x1 -> x2, Pallas kernels: 79.7 us -> 71.5 us  [the longest x1 70.1 us: per_device(): pl.pallas_call(kernel, out_shape=tuple((pltpu.VMEM(shape, kind) for shape...]
    unnamed x11 -> x0, local copies, waits for them, and re-layouts: 6.85 us -> none
where the time goes in v2:
time: 72.2 us; the launch traced here: 72.1 us
  Pallas kernels  71.5 us (99%)
    pallas_call x1, Pallas kernels, per_device(): pl.pallas_call(kernel, out_shape=tuple((pltpu.VMEM(shape, kind) for shape...  70.1 us

profile of v2, /device:TPU:1, one launch (start us, length us, event | category | flops | bytes accessed | tf_op | source)
XLA Modules:
  0.0 72.1 jit_solution(13378865170327482034)
XLA Ops:
  0.6 70.1 %soft_moe_backward.1 = (bf16[256,256]{1,0:T(8,128)(2,1)S(1)}, f32[2,32]{1,0:T(2,128)S(1)}, bf16[2,2048,128]{2,1,0:T(8,128)(2,1)S(1)}, bf16[2,128,2048]{2,1,0:T(8,128)(2,1)S(1)}) custom-call(bf16[2,2048]{1,0:T(2,128)(2,1)} %bitcast.2, bf16[256,256]{1,0:T(8,128)(2,1)} %tokens_hbm.1, bf16[256,256]{1,0:T(8,128)(2,1)} %cotan_hbm.1, ...), custom_call_target="tpu_custom_call" | custom-call | tf_op jit(solution)/shard_map/soft_moe_backward/pallas_call | solution.py:329
  70.7 1.4 %write_out.1 = (bf16[256,256]{1,0:T(8,128)(2,1)}, f32[2,32]{1,0:T(2,128)}, bf16[2,2048,128]{2,1,0:T(8,128)(2,1)}, bf16[2,128,2048]{2,1,0:T(8,128)(2,1)}) custom-call(bf16[256,256]{1,0:T(8,128)(2,1)S(1)} %get-tuple-element.12.refs_0_, f32[2,32]{1,0:T(2,128)S(1)} %get-tuple-element.13.refs_1_, bf16[2,2048,128]{2,1,0:T(8,128)(2,1)S(1)} %get-tuple-element.14.refs_2_, ...), custom_call_target="tpu_custom_call" | custom-call | tf_op jit(solution)/shard_map/write_out/pallas_call | solution.py:355

commit v3 on v2

v3 whole, which is shorter than its diff:
```python
import jax
import jax.numpy as jnp
from jax import lax
from jax.experimental import pallas as pl
from jax.experimental.pallas import tpu as pltpu
from jax.sharding import PartitionSpec as P

MESH = pl.DeviceIdType.MESH
F32, BF16 = jnp.float32, jnp.bfloat16
ROOT_2_PI, CUBE = 0.7978845608, 0.044715
EXP_FAR = ((1, 2), (1, 1), (1, 3), (1, 0), (0, 2), (0, 1), (0, 3))
PAIR_FAR = (4, 3, 5, 2, 6, 1, 7)
MEMBER_FAR = (7, 5, 6, 3, 4, 1, 2)


def dot(lhs, rhs, lhs_dim, rhs_dim):
    return lax.dot_general(
        lhs, rhs, (((lhs_dim,), (rhs_dim,)), ((), ())), preferred_element_type=F32
    )


def kernel(
    keys_hbm, tokens_hbm, cotan_hbm, win_hbm, wout_hbm,
    token_grad_ref, key_ref, in_grad, out_grad,
    key_raw, tok, cot, win, wout,
    key_src, key_buf, log_src, log_buf, c1_src, c1_buf, z_src, z_buf, d_buf,
    e1_src, e1_buf, e2_src, e2_buf, e3_src, e3_buf, g_src, g_buf, h_src, h_buf,
    win_by, win_to, wout_by, wout_to,
    load_sem, meet_sem, near_sem, send_sem, recv_sem,
):
    i, e = lax.axis_index("seq"), lax.axis_index("exp")
    x_lo, z, core = i // 32, (i // 2) % 16, i % 2
    pair, own = z // 2, 2 * (x_lo * 2 + core) + z % 2

    def seq_of(member, pair_at):
        return (member // 4) * 32 + (pair_at * 2 + member % 2) * 2 + (member // 2) % 2

    loads = [
        pltpu.make_async_copy(src, dst, load_sem.at[n])
        for n, (src, dst) in enumerate(
            ((keys_hbm, key_raw), (tokens_hbm, tok), (cotan_hbm, cot), (win_hbm, win), (wout_hbm, wout))
        )
    ]
    for load in loads:
        load.start()

    def exp_at(step):
        return (e // 4 + step[0]) % 2 * 4 + (e + step[1]) % 4

    def member(step):
        return (
            (own // 4 + step // 4) % 2 * 4 + (own // 2 + step // 2) % 2 * 2 + (own + step) % 2
        )

    def signal(sem, seq_at, exp_at):
        pl.semaphore_signal(sem, 1, device_id=(seq_at, exp_at), device_id_type=MESH)

    def meet(step):
        signal(meet_sem.at[step], seq_of(own, (pair + 2**step) % 8), e)
        signal(meet_sem.at[step], seq_of(own, (pair + 8 - 2**step) % 8), e)

    def met(step):
        pl.semaphore_wait(meet_sem.at[step], 2)

    barrier = pltpu.get_barrier_semaphore()
    for step in EXP_FAR:
        signal(barrier, i, exp_at(step))
    for step in MEMBER_FAR:
        signal(barrier, seq_of(member(step), pair), e)
    for k in (1, 7):
        signal(barrier, seq_of(own, (pair + k) % 8), e)
    loads[0].wait()
    keys_wide = key_raw[...].astype(F32)
    for k in range(8):
        key_src[k] = keys_wide[:, 256 * k : 256 * k + 256]
    pl.semaphore_wait(barrier, 16)

    def send(phase, src, dst, seq_at, exp_at):
        pltpu.make_async_remote_copy(
            src, dst, send_sem.at[phase], recv_sem.at[phase],
            device_id=(seq_at, exp_at), device_id_type=MESH,
        ).start()

    def send_or_keep(phase, here, src, dst, seq_at, exp_at):
        @pl.when(here)
        def _():
            pltpu.make_async_copy(src, dst, recv_sem.at[phase]).start()

        @pl.when(jnp.logical_not(here))
        def _():
            send(phase, src, dst, seq_at, exp_at)

    def arrive(phase, ref):
        pltpu.make_async_copy(ref, ref, recv_sem.at[phase]).wait()

    def sent(phase, ref):
        pltpu.make_async_copy(ref, ref, send_sem.at[phase]).wait()

    def sent_some(phase, here, ref, count):
        @pl.when(here)
        def _():
            sent(phase, ref.at[pl.ds(0, count - 1)])

        @pl.when(jnp.logical_not(here))
        def _():
            sent(phase, ref)

    for step in EXP_FAR:
        to = exp_at(step)
        send(0, key_src.at[to], key_buf.at[e], i, to)
    meet(0)
    key_buf[e] = key_src[e]
    loads[1].wait()
    arrive(0, key_buf.at[pl.ds(0, 7)])
    keys = key_buf[...].reshape(16, 256).astype(BF16)

    log_src[...] = dot(keys, tok[...], 1, 1)
    for step in EXP_FAR:
        to = exp_at(step)
        send(1, log_src, log_buf.at[e], i, to)
    met(0)
    meet(1)
    log_buf[e] = log_src[...]
    loads[2].wait()
    arrive(1, log_buf.at[pl.ds(0, 7)])
    logits = log_buf[0]
    for k in range(1, 8):
        logits = logits + log_buf[k]

    peak = jnp.max(logits, axis=1, keepdims=True)
    weight_b = jnp.exp(logits - peak).astype(BF16)
    weight = weight_b.astype(F32)
    total = jnp.sum(weight, axis=1, keepdims=True)
    lse = peak + jnp.log(total)
    row_exp = jnp.exp(logits - jnp.max(logits, axis=0, keepdims=True))
    combine = row_exp / jnp.sum(row_exp, axis=0, keepdims=True)

    slot_part = dot(weight_b, tok[...], 1, 0) / total
    gout_part = dot(combine.astype(BF16), cot[...], 1, 0) * 8.0
    lse_wide = jnp.broadcast_to(lse, (16, 128))
    for b in range(8):
        c1_src[b, 0:2, 0:256] = slot_part[2 * b : 2 * b + 2]
        c1_src[b, 2:4, 0:256] = gout_part[2 * b : 2 * b + 2]
        c1_src[b, 0:2, 256:384] = lse_wide[2 * b : 2 * b + 2]
        c1_src[b, 2:4, 256:384] = jnp.zeros((2, 128), F32)
    home = seq_of(e, pair)
    c1_here = own == e
    for step in EXP_FAR:
        to = exp_at(step)
        send(2, c1_src.at[to], c1_buf.at[own], home, to)
    send_or_keep(2, c1_here, c1_src.at[e], c1_buf.at[own], home, e)
    share = weight / total
    met(1)
    arrive(2, c1_buf)
    def merged(buf):
        top = buf[0, :, 256:384]
        for n in range(1, 8):
            top = jnp.maximum(top, buf[n, :, 256:384])
        norm = jnp.zeros((4, 128), F32)
        low, high = jnp.zeros((4, 128), F32), jnp.zeros((4, 128), F32)
        for n in range(8):
            scale = jnp.exp(buf[n, :, 256:384] - top)
            norm = norm + scale
            low = low + scale * buf[n, :, 0:128]
            high = high + scale * buf[n, :, 128:256]
        return low, high, norm, top + jnp.log(norm)

    row4 = lax.broadcasted_iota(jnp.int32, (4, 256), 0)
    first = row4 < 2
    first_tile = first[:, 0:128]
    low, high, norm, lse_all = merged(c1_buf)
    norm = jnp.where(first_tile, norm, 1.0)
    z_src[:, 0:128] = low / norm
    z_src[:, 128:256] = high / norm
    z_src[:, 256:384] = jnp.where(first_tile, lse_all, 0.0)

    for k in PAIR_FAR:
        send(3, z_src, z_buf.at[pair], seq_of(own, (pair + k) % 8), e)
    z_buf[pair] = z_src[...]
    loads[3].wait()
    loads[4].wait()
    for n in range(8):
        at = n * 256
        pair_in = jnp.concatenate([win[0, at : at + 256, :], win[1, at : at + 256, :]], axis=1)
        win_by[n] = pair_in
        win_to[n] = pair_in.T
        pair_out = wout[:, :, at : at + 256].reshape(256, 256)
        wout_to[n] = pair_out
        wout_by[n] = pair_out.T
    arrive(3, z_buf.at[pl.ds(0, 7)])
    low, high, norm, lse_all = merged(z_buf)
    chunk = jnp.concatenate([low / norm, high / norm], axis=1)

    d_buf[own] = chunk
    for step in MEMBER_FAR:
        pltpu.make_async_remote_copy(
            d_buf.at[own], d_buf.at[own], send_sem.at[4], near_sem.at[step],
            device_id=(seq_of(member(step), pair), e), device_id_type=MESH,
        ).start()
    vec = chunk.astype(BF16)
    pre = dot(vec, win_by[own], 1, 0)
    grad_hidden = dot(vec, wout_by[own], 1, 0)
    for step in MEMBER_FAR[::-1]:
        n = member(step)
        pltpu.make_async_copy(d_buf.at[n], d_buf.at[n], near_sem.at[step]).wait()
        vec = d_buf[n].astype(BF16)
        pre = pre + dot(vec, win_by[n], 1, 0)
        grad_hidden = grad_hidden + dot(vec, wout_by[n], 1, 0)
    pre, grad_hidden = pre[0:2], grad_hidden[2:4]
    tanh = jnp.tanh(ROOT_2_PI * (pre + CUBE * pre * pre * pre))
    hidden = 0.5 * pre * (1.0 + tanh)
    slope = 0.5 * (1.0 + tanh) + 0.5 * pre * (1.0 - tanh * tanh) * ROOT_2_PI * (
        1.0 + 3.0 * CUBE * pre * pre
    )
    lane4 = lax.broadcasted_iota(jnp.int32, (4, 256), 1)
    both = jnp.concatenate([grad_hidden * slope, hidden], axis=0)
    both = jnp.where((lane4 // 128) == (row4 % 2), both, 0.0)
    both_b = both.astype(BF16)

    def partial(n):
        return jnp.where(first, dot(both_b, win_to[n], 1, 0), dot(both_b, wout_to[n], 1, 0))

    for step in MEMBER_FAR:
        to = member(step)
        e1_src[step] = partial(to)
        send(5, e1_src.at[step], e1_buf.at[step], seq_of(to, pair), e)
    full = partial(own)
    arrive(5, e1_buf.at[pl.ds(1, 7)])
    for n in range(1, 8):
        full = full + e1_buf[n]
    e2_src[...] = full
    for k in PAIR_FAR:
        send(6, e2_src, e2_buf.at[pair], seq_of(own, (pair + k) % 8), e)
    e2_buf[pair] = full

    pre_rows = jnp.where(first, both, 0.0).astype(BF16)
    hid_rows = jnp.where(first, 0.0, both).astype(BF16)
    for n in range(8):
        at = n * 256
        vec = d_buf[n].astype(BF16)
        block = dot(vec, pre_rows, 0, 0).astype(BF16)
        in_grad[0, at : at + 256, :] = block[:, 0:128]
        in_grad[1, at : at + 256, :] = block[:, 128:256]
        block = dot(hid_rows, vec, 0, 0).astype(BF16)
        out_grad[:, :, at : at + 256] = block.reshape(2, 128, 256)

    arrive(6, e2_buf.at[pl.ds(0, 7)])
    full = e2_buf[0]
    for n in range(1, 8):
        full = full + e2_buf[n]
    full = full.astype(BF16).astype(F32)
    inner = jnp.sum(full * chunk, axis=1, keepdims=True)
    e3_src[0] = full[0:2]
    e3_src[1] = full[2:4]
    e3_src[2] = jnp.concatenate([lse_all, lse_all], axis=1)[0:2]
    e3_src[3] = jnp.broadcast_to(inner, (4, 256))[0:2]

    for step in MEMBER_FAR:
        send(7, e3_src, e3_buf.at[e], seq_of(member(step), pair), own)
    send_or_keep(7, c1_here, e3_src, e3_buf.at[e], i, own)
    arrive(7, e3_buf)

    def rows_of(kind):
        return e3_buf[:, kind].reshape(16, 256)

    gsi_b = rows_of(0).astype(BF16)
    grad_combine = dot(rows_of(1).astype(BF16), cot[...], 1, 1)
    grad_dispatch = dot(gsi_b, tok[...], 1, 1) - rows_of(3)
    dispatch = share * jnp.exp(lse - rows_of(2))
    combine_row = jnp.sum(combine * grad_combine, axis=0, keepdims=True)
    grad_part = dispatch * grad_dispatch + combine * (grad_combine - combine_row)
    g_src[...] = grad_part
    for step in EXP_FAR:
        send(8, g_src, g_buf.at[e], i, exp_at(step))
    g_buf[e] = grad_part
    arrive(8, g_buf.at[pl.ds(0, 7)])
    grads = g_buf[0]
    for k in range(1, 8):
        grads = grads + g_buf[k]
    grad_logits_b = grads.astype(BF16)

    key_part = dot(grad_logits_b, tok[...], 1, 0)
    lane = lax.broadcasted_iota(jnp.int32, (16, 128), 1)
    for a in range(8):
        own = (key_part if a == 0 else pltpu.roll(key_part, 256 - 32 * a, 1))[:, 0:128]
        odd = pltpu.roll(pltpu.roll(own, 32, 1), 15, 0)
        row = jnp.where(lane < 32, own, odd)
        for b in range(8):
            h_src[a * 8 + b] = row[2 * b : 2 * b + 1]
    h_here = i // 8 == e
    for step in EXP_FAR + ((0, 0),):
        b = exp_at(step)
        for k in list(range(1, 8)) + [0]:
            a = (i + k) % 8
            if k == 0 and step == (0, 0):
                send_or_keep(9, h_here, h_src.at[a * 8 + b], h_buf.at[i], 8 * e + a, b)
            else:
                send(9, h_src.at[a * 8 + b], h_buf.at[i], 8 * e + a, b)

    left = jnp.concatenate([dispatch.astype(BF16), grad_logits_b], axis=0)
    right = jnp.concatenate([gsi_b, keys], axis=0)
    token_grad_ref[...] = dot(left, right, 0, 0).astype(BF16)
    arrive(9, h_buf)
    rows = h_buf[0]
    for n in range(1, 64):
        rows = rows + h_buf[n]
    key_ref[...] = jnp.concatenate([rows[:, 0:32], rows[:, 32:64]], axis=0)

    sent(0, key_buf.at[pl.ds(0, 7)])
    sent(1, log_buf.at[pl.ds(0, 7)])
    sent_some(2, c1_here, c1_src, 8)
    sent(3, z_buf.at[pl.ds(0, 7)])
    sent(4, d_buf.at[pl.ds(0, 7)])
    sent(5, e1_buf.at[pl.ds(0, 7)])
    sent(6, e2_buf.at[pl.ds(0, 7)])
    sent_some(7, c1_here, e3_buf, 8)
    sent(8, g_buf.at[pl.ds(0, 7)])
    sent_some(9, h_here, h_buf, 64)


def write_out(*refs):
    sems = refs[-1]
    pieces = []
    for src, dst in zip(refs[2:4], refs[6:8]):
        rows = src.shape[1] // 4
        for n in range(2):
            for m in range(4):
                part = pl.ds(m * rows, rows)
                pieces.append((src.at[n, part], dst.at[n, part]))
    pieces += list(zip(refs[0:2], refs[4:6]))
    copies = [pltpu.make_async_copy(src, dst, sems.at[n]) for n, (src, dst) in enumerate(pieces)]
    for copy in copies:
        copy.start()
    for copy in copies:
        copy.wait()


def per_device(tokens, cotangent, slot_keys, expert_in, expert_out):
    any_space = pl.BlockSpec(memory_space=pl.ANY)
    buf = pltpu.VMEM
    outs = (
        ((256, 256), BF16), ((2, 32), F32), ((2, 2048, 128), BF16), ((2, 128, 2048), BF16)
    )
    big = [
        pltpu.with_memory_space_constraint(value, pltpu.HBM)
        for value in (slot_keys.T, tokens, cotangent, expert_in, expert_out)
    ]
    held = pl.pallas_call(
        kernel,
        out_shape=tuple(pltpu.VMEM(shape, kind) for shape, kind in outs),
        in_specs=[any_space] * 5,
        scratch_shapes=[
            buf((2, 2048), BF16), buf((256, 256), BF16), buf((256, 256), BF16),
            buf((2, 2048, 128), BF16), buf((2, 128, 2048), BF16),
            buf((8, 2, 256), F32), buf((8, 2, 256), F32),
            buf((16, 256), F32), buf((8, 16, 256), F32),
            buf((8, 4, 384), F32), buf((8, 4, 384), F32),
            buf((4, 384), F32), buf((8, 4, 384), F32),
            buf((8, 4, 256), F32),
            buf((8, 4, 256), F32), buf((8, 4, 256), F32),
            buf((4, 256), F32), buf((8, 4, 256), F32),
            buf((4, 2, 256), F32), buf((8, 4, 2, 256), F32),
            buf((16, 256), F32), buf((8, 16, 256), F32),
            buf((64, 1, 128), F32), buf((64, 1, 128), F32),
            buf((8, 256, 256), BF16), buf((8, 256, 256), BF16),
            buf((8, 256, 256), BF16), buf((8, 256, 256), BF16),
            pltpu.SemaphoreType.DMA((5,)),
            pltpu.SemaphoreType.REGULAR((2,)), pltpu.SemaphoreType.DMA((8,)),
            pltpu.SemaphoreType.DMA((10,)), pltpu.SemaphoreType.DMA((10,)),
        ],
        compiler_params=pltpu.CompilerParams(
            collective_id=0, has_side_effects=True, vmem_limit_bytes=32 * 2**20
        ),
        name="soft_moe_backward",
    )(*big)
    token_grad, key_grad, in_grad, out_grad = pl.pallas_call(
        write_out,
        out_shape=tuple(pltpu.HBM(shape, kind) for shape, kind in outs),
        in_specs=[any_space] * 4,
        out_specs=(any_space,) * 4,
        scratch_shapes=[pltpu.SemaphoreType.DMA((18,))],
        compiler_params=pltpu.CompilerParams(vmem_limit_bytes=2**20),
        name="write_out",
    )(*held)
    return (token_grad, key_grad.T, in_grad, out_grad)


def solution(mesh):
    return jax.shard_map(
        per_device,
        mesh=mesh,
        in_specs=(
            P("seq", "exp"),
            P("seq", "exp"),
            P(None, "exp"),
            P("exp", None, "seq"),
            P("exp", "seq", None),
        ),
        out_specs=(P("seq", "exp"), P("seq", "exp"), P("exp", None, "seq"), P("exp", "seq", None)),
        check_vma=False,
    )
```

time: 72.2 us -> 70.8 us (0.981)
  Pallas kernels: 71.5 us -> 70 us
    pallas_call x1, Pallas kernels: 70.1 us -> 68.5 us  [per_device(): pl.pallas_call(kernel, out_shape=tuple((pltpu.VMEM(shape, kind) for shape...]
where the time goes in v3:
time: 70.8 us; the launch traced here: 70.6 us
  Pallas kernels  70 us (99%)
    pallas_call x1, Pallas kernels, per_device(): pl.pallas_call(kernel, out_shape=tuple((pltpu.VMEM(shape, kind) for shape...  68.5 us
    pallas_call x1, Pallas kernels, per_device(): pl.pallas_call(write_out, out_shape=tuple((pltpu.HBM(shape, kind) for sha...  1.5 us

profile of v3, /device:TPU:1, one launch (start us, length us, event | category | flops | bytes accessed | tf_op | source)
XLA Modules:
  0.0 70.6 jit_solution(6380185807486131577)
XLA Ops:
  0.6 68.5 %soft_moe_backward.1 = (bf16[256,256]{1,0:T(8,128)(2,1)S(1)}, f32[2,32]{1,0:T(2,128)S(1)}, bf16[2,2048,128]{2,1,0:T(8,128)(2,1)S(1)}, bf16[2,128,2048]{2,1,0:T(8,128)(2,1)S(1)}) custom-call(bf16[2,2048]{1,0:T(2,128)(2,1)} %bitcast.2, bf16[256,256]{1,0:T(8,128)(2,1)} %tokens_hbm.1, bf16[256,256]{1,0:T(8,128)(2,1)} %cotan_hbm.1, ...), custom_call_target="tpu_custom_call" | custom-call | tf_op jit(solution)/shard_map/soft_moe_backward/pallas_call | solution.py:348
  69.1 1.5 %write_out.1 = (bf16[256,256]{1,0:T(8,128)(2,1)}, f32[2,32]{1,0:T(2,128)}, bf16[2,2048,128]{2,1,0:T(8,128)(2,1)}, bf16[2,128,2048]{2,1,0:T(8,128)(2,1)}) custom-call(bf16[256,256]{1,0:T(8,128)(2,1)S(1)} %get-tuple-element.12.refs_0_, f32[2,32]{1,0:T(2,128)S(1)} %get-tuple-element.13.refs_1_, bf16[2,2048,128]{2,1,0:T(8,128)(2,1)S(1)} %get-tuple-element.14.refs_2_, ...), custom_call_target="tpu_custom_call" | custom-call | tf_op jit(solution)/shard_map/write_out/pallas_call | solution.py:376

commit v4 on v3

--- a/solution.py
+++ b/solution.py
@@ -25,6 +25,7 @@
     key_raw, tok, cot, win, wout,
     key_src, key_buf, log_src, log_buf, c1_src, c1_buf, z_src, z_buf, d_buf,
     e1_src, e1_buf, e2_src, e2_buf, e3_src, e3_buf, g_src, g_buf, h_src, h_buf,
+    lse_src, lse_buf, tok_t, cot_t,
     win_by, win_to, wout_by, wout_to,
     load_sem, meet_sem, near_sem, send_sem, recv_sem,
 ):
@@ -73,6 +74,8 @@
     keys_wide = key_raw[...].astype(F32)
     for k in range(8):
         key_src[k] = keys_wide[:, 256 * k : 256 * k + 256]
+    loads[1].wait()
+    tok_t[...] = tok[...].T
     pl.semaphore_wait(barrier, 16)
 
     def send(phase, src, dst, seq_at, exp_at):
@@ -93,6 +96,15 @@
     def arrive(phase, ref):
         pltpu.make_async_copy(ref, ref, recv_sem.at[phase]).wait()
 
+    def send_near(step, src, dst, seq_at, exp_at):
+        pltpu.make_async_remote_copy(
+            src, dst, send_sem.at[4], near_sem.at[step],
+            device_id=(seq_at, exp_at), device_id_type=MESH,
+        ).start()
+
+    def arrive_near(step, ref):
+        pltpu.make_async_copy(ref, ref, near_sem.at[step]).wait()
+
     def sent(phase, ref):
         pltpu.make_async_copy(ref, ref, send_sem.at[phase]).wait()
 
@@ -110,11 +122,10 @@
         send(0, key_src.at[to], key_buf.at[e], i, to)
     meet(0)
     key_buf[e] = key_src[e]
-    loads[1].wait()
     arrive(0, key_buf.at[pl.ds(0, 7)])
     keys = key_buf[...].reshape(16, 256).astype(BF16)
 
-    log_src[...] = dot(keys, tok[...], 1, 1)
+    log_src[...] = dot(keys, tok_t[...], 1, 0)
     for step in EXP_FAR:
         to = exp_at(step)
         send(1, log_src, log_buf.at[e], i, to)
@@ -187,22 +198,20 @@
         pair_out = wout[:, :, at : at + 256].reshape(256, 256)
         wout_to[n] = pair_out
         wout_by[n] = pair_out.T
+    cot_t[...] = cot[...].T
     arrive(3, z_buf.at[pl.ds(0, 7)])
     low, high, norm, lse_all = merged(z_buf)
     chunk = jnp.concatenate([low / norm, high / norm], axis=1)
 
     d_buf[own] = chunk
     for step in MEMBER_FAR:
-        pltpu.make_async_remote_copy(
-            d_buf.at[own], d_buf.at[own], send_sem.at[4], near_sem.at[step],
-            device_id=(seq_of(member(step), pair), e), device_id_type=MESH,
-        ).start()
+        send_near(step, d_buf.at[own], d_buf.at[own], seq_of(member(step), pair), e)
     vec = chunk.astype(BF16)
     pre = dot(vec, win_by[own], 1, 0)
     grad_hidden = dot(vec, wout_by[own], 1, 0)
     for step in MEMBER_FAR[::-1]:
         n = member(step)
-        pltpu.make_async_copy(d_buf.at[n], d_buf.at[n], near_sem.at[step]).wait()
+        arrive_near(step, d_buf.at[n])
         vec = d_buf[n].astype(BF16)
         pre = pre + dot(vec, win_by[n], 1, 0)
         grad_hidden = grad_hidden + dot(vec, wout_by[n], 1, 0)
@@ -233,6 +242,10 @@
         send(6, e2_src, e2_buf.at[pair], seq_of(own, (pair + k) % 8), e)
     e2_buf[pair] = full
 
+    lse_src[...] = lse_all[0:2]
+    for step in EXP_FAR:
+        send(10, lse_src, lse_buf.at[e], i, exp_at(step))
+    lse_buf[e] = lse_all[0:2]
     pre_rows = jnp.where(first, both, 0.0).astype(BF16)
     hid_rows = jnp.where(first, 0.0, both).astype(BF16)
     for n in range(8):
@@ -244,6 +257,9 @@
         block = dot(hid_rows, vec, 0, 0).astype(BF16)
         out_grad[:, :, at : at + 256] = block.reshape(2, 128, 256)
 
+    arrive(10, lse_buf.at[pl.ds(0, 7)])
+    lse_rows = lse_buf[...].reshape(16, 128)
+    dispatch = share * jnp.exp(lse - jnp.concatenate([lse_rows, lse_rows], axis=1))
     arrive(6, e2_buf.at[pl.ds(0, 7)])
     full = e2_buf[0]
     for n in range(1, 8):
@@ -252,8 +268,7 @@
     inner = jnp.sum(full * chunk, axis=1, keepdims=True)
     e3_src[0] = full[0:2]
     e3_src[1] = full[2:4]
-    e3_src[2] = jnp.concatenate([lse_all, lse_all], axis=1)[0:2]
-    e3_src[3] = jnp.broadcast_to(inner, (4, 256))[0:2]
+    e3_src[2] = jnp.broadcast_to(inner, (4, 256))[0:2]
 
     for step in MEMBER_FAR:
         send(7, e3_src, e3_buf.at[e], seq_of(member(step), pair), own)
@@ -264,19 +279,19 @@
         return e3_buf[:, kind].reshape(16, 256)
 
     gsi_b = rows_of(0).astype(BF16)
-    grad_combine = dot(rows_of(1).astype(BF16), cot[...], 1, 1)
-    grad_dispatch = dot(gsi_b, tok[...], 1, 1) - rows_of(3)
-    dispatch = share * jnp.exp(lse - rows_of(2))
+    grad_combine = dot(rows_of(1).astype(BF16), cot_t[...], 1, 0)
+    grad_dispatch = dot(gsi_b, tok_t[...], 1, 0) - rows_of(2)
     combine_row = jnp.sum(combine * grad_combine, axis=0, keepdims=True)
     grad_part = dispatch * grad_dispatch + combine * (grad_combine - combine_row)
+    grad_part = grad_part.astype(BF16)
     g_src[...] = grad_part
     for step in EXP_FAR:
         send(8, g_src, g_buf.at[e], i, exp_at(step))
     g_buf[e] = grad_part
     arrive(8, g_buf.at[pl.ds(0, 7)])
-    grads = g_buf[0]
+    grads = g_buf[0].astype(F32)
     for k in range(1, 8):
-        grads = grads + g_buf[k]
+        grads = grads + g_buf[k].astype(F32)
     grad_logits_b = grads.astype(BF16)
 
     key_part = dot(grad_logits_b, tok[...], 1, 0)
@@ -316,19 +331,15 @@
     sent_some(7, c1_here, e3_buf, 8)
     sent(8, g_buf.at[pl.ds(0, 7)])
     sent_some(9, h_here, h_buf, 64)
+    sent(10, lse_buf.at[pl.ds(0, 7)])
 
 
 def write_out(*refs):
     sems = refs[-1]
-    pieces = []
-    for src, dst in zip(refs[2:4], refs[6:8]):
-        rows = src.shape[1] // 4
-        for n in range(2):
-            for m in range(4):
-                part = pl.ds(m * rows, rows)
-                pieces.append((src.at[n, part], dst.at[n, part]))
-    pieces += list(zip(refs[0:2], refs[4:6]))
-    copies = [pltpu.make_async_copy(src, dst, sems.at[n]) for n, (src, dst) in enumerate(pieces)]
+    count = (len(refs) - 1) // 2
+    copies = [
+        pltpu.make_async_copy(refs[n], refs[count + n], sems.at[n]) for n in range(count)
+    ]
     for copy in copies:
         copy.start()
     for copy in copies:
@@ -359,14 +370,16 @@
             buf((8, 4, 256), F32),
             buf((8, 4, 256), F32), buf((8, 4, 256), F32),
             buf((4, 256), F32), buf((8, 4, 256), F32),
-            buf((4, 2, 256), F32), buf((8, 4, 2, 256), F32),
-            buf((16, 256), F32), buf((8, 16, 256), F32),
+            buf((3, 2, 256), F32), buf((8, 3, 2, 256), F32),
+            buf((16, 256), BF16), buf((8, 16, 256), BF16),
             buf((64, 1, 128), F32), buf((64, 1, 128), F32),
+            buf((2, 128), F32), buf((8, 2, 128), F32),
+            buf((256, 256), BF16), buf((256, 256), BF16),
             buf((8, 256, 256), BF16), buf((8, 256, 256), BF16),
             buf((8, 256, 256), BF16), buf((8, 256, 256), BF16),
             pltpu.SemaphoreType.DMA((5,)),
             pltpu.SemaphoreType.REGULAR((2,)), pltpu.SemaphoreType.DMA((8,)),
-            pltpu.SemaphoreType.DMA((10,)), pltpu.SemaphoreType.DMA((10,)),
+            pltpu.SemaphoreType.DMA((11,)), pltpu.SemaphoreType.DMA((11,)),
         ],
         compiler_params=pltpu.CompilerParams(
             collective_id=0, has_side_effects=True, vmem_limit_bytes=32 * 2**20
@@ -378,7 +391,7 @@
         out_shape=tuple(pltpu.HBM(shape, kind) for shape, kind in outs),
         in_specs=[any_space] * 4,
         out_specs=(any_space,) * 4,
-        scratch_shapes=[pltpu.SemaphoreType.DMA((18,))],
+        scratch_shapes=[pltpu.SemaphoreType.DMA((4,))],
         compiler_params=pltpu.CompilerParams(vmem_limit_bytes=2**20),
         name="write_out",
     )(*held)

time: 70.8 us -> 70.3 us (level)
  no operation moved by 1% of the time
where the time goes in v4:
time: 70.3 us; the launch traced here: 70.1 us
  Pallas kernels  69.5 us (99%)
    pallas_call x1, Pallas kernels, per_device(): pl.pallas_call(kernel, out_shape=tuple((pltpu.VMEM(shape, kind) for shape...  68.1 us

profile of v4, /device:TPU:1, one launch (start us, length us, event | category | flops | bytes accessed | tf_op | source)
XLA Modules:
  0.0 70.1 jit_solution(6203299217721201037)
XLA Ops:
  0.6 68.1 %soft_moe_backward.1 = (bf16[256,256]{1,0:T(8,128)(2,1)S(1)}, f32[2,32]{1,0:T(2,128)S(1)}, bf16[2,2048,128]{2,1,0:T(8,128)(2,1)S(1)}, bf16[2,128,2048]{2,1,0:T(8,128)(2,1)S(1)}) custom-call(bf16[2,2048]{1,0:T(2,128)(2,1)} %bitcast.2, bf16[256,256]{1,0:T(8,128)(2,1)} %tokens_hbm.1, bf16[256,256]{1,0:T(8,128)(2,1)} %cotan_hbm.1, ...), custom_call_target="tpu_custom_call" | custom-call | tf_op jit(solution)/shard_map/soft_moe_backward/pallas_call | solution.py:359
  68.7 1.4 %write_out.1 = (bf16[256,256]{1,0:T(8,128)(2,1)}, f32[2,32]{1,0:T(2,128)}, bf16[2,2048,128]{2,1,0:T(8,128)(2,1)}, bf16[2,128,2048]{2,1,0:T(8,128)(2,1)}) custom-call(bf16[256,256]{1,0:T(8,128)(2,1)S(1)} %get-tuple-element.12.refs_0_, f32[2,32]{1,0:T(2,128)S(1)} %get-tuple-element.13.refs_1_, bf16[2,2048,128]{2,1,0:T(8,128)(2,1)S(1)} %get-tuple-element.14.refs_2_, ...), custom_call_target="tpu_custom_call" | custom-call | tf_op jit(solution)/shard_map/write_out/pallas_call | solution.py:389

commit v5 on v4

--- a/solution.py
+++ b/solution.py
@@ -25,7 +25,7 @@
     key_raw, tok, cot, win, wout,
     key_src, key_buf, log_src, log_buf, c1_src, c1_buf, z_src, z_buf, d_buf,
     e1_src, e1_buf, e2_src, e2_buf, e3_src, e3_buf, g_src, g_buf, h_src, h_buf,
-    lse_src, lse_buf, tok_t, cot_t,
+    lse_src, lse_buf, tok_t, cot_t, tok_pair,
     win_by, win_to, wout_by, wout_to,
     load_sem, meet_sem, near_sem, send_sem, recv_sem,
 ):
@@ -53,6 +53,9 @@
             (own // 4 + step // 4) % 2 * 4 + (own // 2 + step // 2) % 2 * 2 + (own + step) % 2
         )
 
+    def key_seq(step):
+        return (x_lo + step[0]) % 2 * 32 + i % 32
+
     def signal(sem, seq_at, exp_at):
         pl.semaphore_signal(sem, 1, device_id=(seq_at, exp_at), device_id_type=MESH)
 
@@ -65,7 +68,7 @@
 
     barrier = pltpu.get_barrier_semaphore()
     for step in EXP_FAR:
-        signal(barrier, i, exp_at(step))
+        signal(barrier, key_seq(step), exp_at(step))
     for step in MEMBER_FAR:
         signal(barrier, seq_of(member(step), pair), e)
     for k in (1, 7):
@@ -119,7 +122,7 @@
 
     for step in EXP_FAR:
         to = exp_at(step)
-        send(0, key_src.at[to], key_buf.at[e], i, to)
+        send(0, key_src.at[to], key_buf.at[e], key_seq(step), to)
     meet(0)
     key_buf[e] = key_src[e]
     arrive(0, key_buf.at[pl.ds(0, 7)])
@@ -199,6 +202,11 @@
         wout_to[n] = pair_out
         wout_by[n] = pair_out.T
     cot_t[...] = cot[...].T
+    for n in range(8):
+        some = tok[:, 32 * n : 32 * n + 32]
+        none = jnp.zeros((256, 32), BF16)
+        tok_pair[0:256, 64 * n : 64 * n + 64] = jnp.concatenate([some, none], axis=1)
+        tok_pair[256:512, 64 * n : 64 * n + 64] = jnp.concatenate([none, some], axis=1)
     arrive(3, z_buf.at[pl.ds(0, 7)])
     low, high, norm, lse_all = merged(z_buf)
     chunk = jnp.concatenate([low / norm, high / norm], axis=1)
@@ -294,23 +302,20 @@
         grads = grads + g_buf[k].astype(F32)
     grad_logits_b = grads.astype(BF16)
 
-    key_part = dot(grad_logits_b, tok[...], 1, 0)
-    lane = lax.broadcasted_iota(jnp.int32, (16, 128), 1)
-    for a in range(8):
-        own = (key_part if a == 0 else pltpu.roll(key_part, 256 - 32 * a, 1))[:, 0:128]
-        odd = pltpu.roll(pltpu.roll(own, 32, 1), 15, 0)
-        row = jnp.where(lane < 32, own, odd)
-        for b in range(8):
-            h_src[a * 8 + b] = row[2 * b : 2 * b + 1]
+    both_slots = jnp.concatenate([grads, pltpu.roll(grads, 15, 0)], axis=1).astype(BF16)
+    rows = dot(both_slots, tok_pair[...], 1, 0)
+    for b in range(8):
+        for n in range(4):
+            h_src[n * 8 + b] = rows[2 * b : 2 * b + 1, 128 * n : 128 * n + 128]
     h_here = i // 8 == e
     for step in EXP_FAR + ((0, 0),):
         b = exp_at(step)
         for k in list(range(1, 8)) + [0]:
             a = (i + k) % 8
             if k == 0 and step == (0, 0):
-                send_or_keep(9, h_here, h_src.at[a * 8 + b], h_buf.at[i], 8 * e + a, b)
+                send_or_keep(9, h_here, h_src.at[a // 2 * 8 + b], h_buf.at[i], 8 * e + a, b)
             else:
-                send(9, h_src.at[a * 8 + b], h_buf.at[i], 8 * e + a, b)
+                send(9, h_src.at[a // 2 * 8 + b], h_buf.at[i], 8 * e + a, b)
 
     left = jnp.concatenate([dispatch.astype(BF16), grad_logits_b], axis=0)
     right = jnp.concatenate([gsi_b, keys], axis=0)
@@ -319,6 +324,7 @@
     rows = h_buf[0]
     for n in range(1, 64):
         rows = rows + h_buf[n]
+    rows = jnp.where(i % 2 == 0, rows[:, 0:64], rows[:, 64:128])
     key_ref[...] = jnp.concatenate([rows[:, 0:32], rows[:, 32:64]], axis=0)
 
     sent(0, key_buf.at[pl.ds(0, 7)])
@@ -372,9 +378,9 @@
             buf((4, 256), F32), buf((8, 4, 256), F32),
             buf((3, 2, 256), F32), buf((8, 3, 2, 256), F32),
             buf((16, 256), BF16), buf((8, 16, 256), BF16),
-            buf((64, 1, 128), F32), buf((64, 1, 128), F32),
+            buf((32, 1, 128), F32), buf((64, 1, 128), F32),
             buf((2, 128), F32), buf((8, 2, 128), F32),
-            buf((256, 256), BF16), buf((256, 256), BF16),
+            buf((256, 256), BF16), buf((256, 256), BF16), buf((512, 512), BF16),
             buf((8, 256, 256), BF16), buf((8, 256, 256), BF16),
             buf((8, 256, 256), BF16), buf((8, 256, 256), BF16),
             pltpu.SemaphoreType.DMA((5,)),

time: 70.3 us -> 69.7 us (level)
  no operation moved by 1% of the time
where the time goes in v5:
time: 69.7 us; the launch traced here: 69.5 us
  Pallas kernels  68.9 us (99%)
    pallas_call x1, Pallas kernels, per_device(): pl.pallas_call(kernel, out_shape=tuple((pltpu.VMEM(shape, kind) for shape...  67.5 us
    pallas_call x1, Pallas kernels, per_device(): pl.pallas_call(write_out, out_shape=tuple((pltpu.HBM(shape, kind) for sha...  1.4 us

profile of v5, /device:TPU:1, one launch (start us, length us, event | category | flops | bytes accessed | tf_op | source)
XLA Modules:
  0.0 69.5 jit_solution(6673374719676484914)
XLA Ops:
  0.6 67.5 %soft_moe_backward.1 = (bf16[256,256]{1,0:T(8,128)(2,1)S(1)}, f32[2,32]{1,0:T(2,128)S(1)}, bf16[2,2048,128]{2,1,0:T(8,128)(2,1)S(1)}, bf16[2,128,2048]{2,1,0:T(8,128)(2,1)S(1)}) custom-call(bf16[2,2048]{1,0:T(2,128)(2,1)} %bitcast.2, bf16[256,256]{1,0:T(8,128)(2,1)} %tokens_hbm.1, bf16[256,256]{1,0:T(8,128)(2,1)} %cotan_hbm.1, ...), custom_call_target="tpu_custom_call" | custom-call | tf_op jit(solution)/shard_map/soft_moe_backward/pallas_call | solution.py:365
  68.1 1.4 %write_out.1 = (bf16[256,256]{1,0:T(8,128)(2,1)}, f32[2,32]{1,0:T(2,128)}, bf16[2,2048,128]{2,1,0:T(8,128)(2,1)}, bf16[2,128,2048]{2,1,0:T(8,128)(2,1)}) custom-call(bf16[256,256]{1,0:T(8,128)(2,1)S(1)} %get-tuple-element.12.refs_0_, f32[2,32]{1,0:T(2,128)S(1)} %get-tuple-element.13.refs_1_, bf16[2,2048,128]{2,1,0:T(8,128)(2,1)S(1)} %get-tuple-element.14.refs_2_, ...), custom_call_target="tpu_custom_call" | custom-call | tf_op jit(solution)/shard_map/write_out/pallas_call | solution.py:395

commit v6 on v5

--- a/solution.py
+++ b/solution.py
@@ -11,6 +11,8 @@
 EXP_FAR = ((1, 2), (1, 1), (1, 3), (1, 0), (0, 2), (0, 1), (0, 3))
 PAIR_FAR = (4, 3, 5, 2, 6, 1, 7)
 MEMBER_FAR = (7, 5, 6, 3, 4, 1, 2)
+QUAD_FAR = (3, 2, 1)
+PLANE_FAR = (8, 7, 9, 6, 10, 5, 11, 4, 12, 3, 13, 2, 14, 1, 15)
 
 
 def dot(lhs, rhs, lhs_dim, rhs_dim):
@@ -26,7 +28,7 @@
     key_src, key_buf, log_src, log_buf, c1_src, c1_buf, z_src, z_buf, d_buf,
     e1_src, e1_buf, e2_src, e2_buf, e3_src, e3_buf, g_src, g_buf, h_src, h_buf,
     lse_src, lse_buf, tok_t, cot_t, tok_pair,
-    win_by, win_to, wout_by, wout_to,
+    w_by, w_to,
     load_sem, meet_sem, near_sem, send_sem, recv_sem,
 ):
     i, e = lax.axis_index("seq"), lax.axis_index("exp")
@@ -36,6 +38,42 @@
     def seq_of(member, pair_at):
         return (member // 4) * 32 + (pair_at * 2 + member % 2) * 2 + (member // 2) % 2
 
+    quad = own // 2
+
+    def plane_seq(quarter, z_at):
+        return quarter // 2 * 32 + z_at * 2 + quarter % 2
+
+    def quarter(step):
+        return (quad // 2 + step // 2) % 2 * 2 + (quad + step) % 2
+
+    def exp_at(step):
+        return (e // 4 + step[0]) % 2 * 4 + (e + step[1]) % 4
+
+    def member(step):
+        return (
+            (own // 4 + step // 4) % 2 * 4 + (own // 2 + step // 2) % 2 * 2 + (own + step) % 2
+        )
+
+    def key_seq(step):
+        return (x_lo + step[0]) % 2 * 32 + i % 32
+
+    def signal(sem, seq_at, exp_at):
+        pl.semaphore_signal(sem, 1, device_id=(seq_at, exp_at), device_id_type=MESH)
+
+    def meet(step):
+        signal(meet_sem.at[step], seq_of(own, (pair + 2**step) % 8), e)
+        signal(meet_sem.at[step], seq_of(own, (pair + 8 - 2**step) % 8), e)
+
+    def met(step):
+        pl.semaphore_wait(meet_sem.at[step], 2)
+
+    barrier = pltpu.get_barrier_semaphore()
+    for step in EXP_FAR:
+        signal(barrier, key_seq(step), exp_at(step))
+    for step in MEMBER_FAR:
+        signal(barrier, seq_of(member(step), pair), e)
+    for k in (1, 7):
+        signal(barrier, seq_of(own, (pair + k) % 8), e)
     loads = [
         pltpu.make_async_copy(src, dst, load_sem.at[n])
         for n, (src, dst) in enumerate(
@@ -44,35 +82,6 @@
     ]
     for load in loads:
         load.start()
-
-    def exp_at(step):
-        return (e // 4 + step[0]) % 2 * 4 + (e + step[1]) % 4
-
-    def member(step):
-        return (
-            (own // 4 + step // 4) % 2 * 4 + (own // 2 + step // 2) % 2 * 2 + (own + step) % 2
-        )
-
-    def key_seq(step):
-        return (x_lo + step[0]) % 2 * 32 + i % 32
-
-    def signal(sem, seq_at, exp_at):
-        pl.semaphore_signal(sem, 1, device_id=(seq_at, exp_at), device_id_type=MESH)
-
-    def meet(step):
-        signal(meet_sem.at[step], seq_of(own, (pair + 2**step) % 8), e)
-        signal(meet_sem.at[step], seq_of(own, (pair + 8 - 2**step) % 8), e)
-
-    def met(step):
-        pl.semaphore_wait(meet_sem.at[step], 2)
-
-    barrier = pltpu.get_barrier_semaphore()
-    for step in EXP_FAR:
-        signal(barrier, key_seq(step), exp_at(step))
-    for step in MEMBER_FAR:
-        signal(barrier, seq_of(member(step), pair), e)
-    for k in (1, 7):
-        signal(barrier, seq_of(own, (pair + k) % 8), e)
     loads[0].wait()
     keys_wide = key_raw[...].astype(F32)
     for k in range(8):
@@ -193,14 +202,16 @@
     z_buf[pair] = z_src[...]
     loads[3].wait()
     loads[4].wait()
-    for n in range(8):
-        at = n * 256
-        pair_in = jnp.concatenate([win[0, at : at + 256, :], win[1, at : at + 256, :]], axis=1)
-        win_by[n] = pair_in
-        win_to[n] = pair_in.T
-        pair_out = wout[:, :, at : at + 256].reshape(256, 256)
-        wout_to[n] = pair_out
-        wout_by[n] = pair_out.T
+    @pl.loop(0, 8)
+    def _(n):
+        at = pl.ds(pl.multiple_of(n * 256, 256), 256)
+        pair_in = jnp.concatenate([win[0, at, :], win[1, at, :]], axis=1)
+        pair_out = wout[:, :, at].reshape(256, 256)
+        w_by[n, :, 0:256] = pair_in
+        w_by[n, :, 256:512] = pair_out.T
+        w_to[n, 0:256, :] = pair_in.T
+        w_to[n, 256:512, :] = pair_out
+
     cot_t[...] = cot[...].T
     for n in range(8):
         some = tok[:, 32 * n : 32 * n + 32]
@@ -215,15 +226,13 @@
     for step in MEMBER_FAR:
         send_near(step, d_buf.at[own], d_buf.at[own], seq_of(member(step), pair), e)
     vec = chunk.astype(BF16)
-    pre = dot(vec, win_by[own], 1, 0)
-    grad_hidden = dot(vec, wout_by[own], 1, 0)
+    wide = dot(vec, w_by[own], 1, 0)
     for step in MEMBER_FAR[::-1]:
         n = member(step)
         arrive_near(step, d_buf.at[n])
         vec = d_buf[n].astype(BF16)
-        pre = pre + dot(vec, win_by[n], 1, 0)
-        grad_hidden = grad_hidden + dot(vec, wout_by[n], 1, 0)
-    pre, grad_hidden = pre[0:2], grad_hidden[2:4]
+        wide = wide + dot(vec, w_by[n], 1, 0)
+    pre, grad_hidden = wide[0:2, 0:256], wide[2:4, 256:512]
     tanh = jnp.tanh(ROOT_2_PI * (pre + CUBE * pre * pre * pre))
     hidden = 0.5 * pre * (1.0 + tanh)
     slope = 0.5 * (1.0 + tanh) + 0.5 * pre * (1.0 - tanh * tanh) * ROOT_2_PI * (
@@ -232,55 +241,64 @@
     lane4 = lax.broadcasted_iota(jnp.int32, (4, 256), 1)
     both = jnp.concatenate([grad_hidden * slope, hidden], axis=0)
     both = jnp.where((lane4 // 128) == (row4 % 2), both, 0.0)
-    both_b = both.astype(BF16)
+    pre_rows = jnp.where(first, both, 0.0).astype(BF16)
+    hid_rows = jnp.where(first, 0.0, both).astype(BF16)
+    rows_wide = jnp.concatenate([pre_rows, hid_rows], axis=1)
 
     def partial(n):
-        return jnp.where(first, dot(both_b, win_to[n], 1, 0), dot(both_b, wout_to[n], 1, 0))
-
-    for step in MEMBER_FAR:
-        to = member(step)
-        e1_src[step] = partial(to)
-        send(5, e1_src.at[step], e1_buf.at[step], seq_of(to, pair), e)
-    full = partial(own)
-    arrive(5, e1_buf.at[pl.ds(1, 7)])
-    for n in range(1, 8):
-        full = full + e1_buf[n]
-    e2_src[...] = full
-    for k in PAIR_FAR:
-        send(6, e2_src, e2_buf.at[pair], seq_of(own, (pair + k) % 8), e)
-    e2_buf[pair] = full
+        return dot(rows_wide, w_to[n], 1, 0)
+
+    for step in QUAD_FAR:
+        to = quarter(step)
+        for h in range(2):
+            e1_src[step, h] = partial(2 * to + h)
+        send(5, e1_src.at[step], e1_buf.at[step], plane_seq(to, z), e)
+    full = [partial(2 * quad + h) for h in range(2)]
+    arrive(5, e1_buf.at[pl.ds(1, 3)])
+    packed = []
+    for h in range(2):
+        some = full[h] + e1_buf[1, h] + (e1_buf[2, h] + e1_buf[3, h])
+        packed += [some[:, 0:128], some[:, 128:256]]
+    packed = jnp.concatenate(packed, axis=0).astype(BF16)
+    e2_src[...] = packed
+    for k in PLANE_FAR:
+        send(6, e2_src, e2_buf.at[z], plane_seq(quad, (z + k) % 16), e)
+    e2_buf[z] = packed
 
     lse_src[...] = lse_all[0:2]
     for step in EXP_FAR:
         send(10, lse_src, lse_buf.at[e], i, exp_at(step))
     lse_buf[e] = lse_all[0:2]
-    pre_rows = jnp.where(first, both, 0.0).astype(BF16)
-    hid_rows = jnp.where(first, 0.0, both).astype(BF16)
-    for n in range(8):
-        at = n * 256
+    @pl.loop(0, 8)
+    def _(n):
+        at = pl.ds(pl.multiple_of(n * 256, 256), 256)
         vec = d_buf[n].astype(BF16)
         block = dot(vec, pre_rows, 0, 0).astype(BF16)
-        in_grad[0, at : at + 256, :] = block[:, 0:128]
-        in_grad[1, at : at + 256, :] = block[:, 128:256]
+        in_grad[0, at, :] = block[:, 0:128]
+        in_grad[1, at, :] = block[:, 128:256]
         block = dot(hid_rows, vec, 0, 0).astype(BF16)
-        out_grad[:, :, at : at + 256] = block.reshape(2, 128, 256)
+        out_grad[:, :, at] = block.reshape(2, 128, 256)
 
     arrive(10, lse_buf.at[pl.ds(0, 7)])
     lse_rows = lse_buf[...].reshape(16, 128)
     dispatch = share * jnp.exp(lse - jnp.concatenate([lse_rows, lse_rows], axis=1))
-    arrive(6, e2_buf.at[pl.ds(0, 7)])
-    full = e2_buf[0]
-    for n in range(1, 8):
-        full = full + e2_buf[n]
-    full = full.astype(BF16).astype(F32)
-    inner = jnp.sum(full * chunk, axis=1, keepdims=True)
-    e3_src[0] = full[0:2]
-    e3_src[1] = full[2:4]
-    e3_src[2] = jnp.broadcast_to(inner, (4, 256))[0:2]
-
-    for step in MEMBER_FAR:
-        send(7, e3_src, e3_buf.at[e], seq_of(member(step), pair), own)
-    send_or_keep(7, c1_here, e3_src, e3_buf.at[e], i, own)
+    arrive(6, e2_buf.at[pl.ds(0, 15)])
+    sums = [e2_buf[n].astype(F32) for n in range(16)]
+    while len(sums) > 1:
+        sums = [sums[n] + sums[n + 1] for n in range(0, len(sums), 2)]
+    packed = sums[0].astype(BF16).astype(F32)
+    for h in range(2):
+        full = jnp.concatenate([packed[8 * h : 8 * h + 4], packed[8 * h + 4 : 8 * h + 8]], axis=1)
+        inner = jnp.sum(full * d_buf[2 * quad + h], axis=1, keepdims=True)
+        e3_src[h, 0] = full[0:2]
+        e3_src[h, 1] = full[2:4]
+        e3_src[h, 2] = jnp.broadcast_to(inner, (4, 256))[0:2]
+
+    for step in QUAD_FAR:
+        for h in range(2):
+            send(7, e3_src.at[h], e3_buf.at[e], plane_seq(quarter(step), z), 2 * quad + h)
+    for h in range(2):
+        send_or_keep(7, 2 * quad + h == e, e3_src.at[h], e3_buf.at[e], i, 2 * quad + h)
     arrive(7, e3_buf)
 
     def rows_of(kind):
@@ -320,24 +338,25 @@
     left = jnp.concatenate([dispatch.astype(BF16), grad_logits_b], axis=0)
     right = jnp.concatenate([gsi_b, keys], axis=0)
     token_grad_ref[...] = dot(left, right, 0, 0).astype(BF16)
-    arrive(9, h_buf)
-    rows = h_buf[0]
-    for n in range(1, 64):
-        rows = rows + h_buf[n]
-    rows = jnp.where(i % 2 == 0, rows[:, 0:64], rows[:, 64:128])
-    key_ref[...] = jnp.concatenate([rows[:, 0:32], rows[:, 32:64]], axis=0)
 
     sent(0, key_buf.at[pl.ds(0, 7)])
     sent(1, log_buf.at[pl.ds(0, 7)])
     sent_some(2, c1_here, c1_src, 8)
     sent(3, z_buf.at[pl.ds(0, 7)])
     sent(4, d_buf.at[pl.ds(0, 7)])
-    sent(5, e1_buf.at[pl.ds(0, 7)])
-    sent(6, e2_buf.at[pl.ds(0, 7)])
-    sent_some(7, c1_here, e3_buf, 8)
+    sent(5, e1_buf.at[pl.ds(0, 3)])
+    sent(6, e2_buf.at[pl.ds(0, 15)])
+    sent_some(7, quad == e // 2, e3_buf, 8)
     sent(8, g_buf.at[pl.ds(0, 7)])
     sent_some(9, h_here, h_buf, 64)
     sent(10, lse_buf.at[pl.ds(0, 7)])
+    arrive(9, h_buf)
+    sums = [h_buf[n] for n in range(64)]
+    while len(sums) > 1:
+        sums = [sums[n] + sums[n + 1] for n in range(0, len(sums), 2)]
+    rows = sums[0]
+    rows = jnp.where(i % 2 == 0, rows[:, 0:64], rows[:, 64:128])
+    key_ref[...] = jnp.concatenate([rows[:, 0:32], rows[:, 32:64]], axis=0)
 
 
 def write_out(*refs):
@@ -374,15 +393,14 @@
             buf((8, 4, 384), F32), buf((8, 4, 384), F32),
             buf((4, 384), F32), buf((8, 4, 384), F32),
             buf((8, 4, 256), F32),
-            buf((8, 4, 256), F32), buf((8, 4, 256), F32),
-            buf((4, 256), F32), buf((8, 4, 256), F32),
-            buf((3, 2, 256), F32), buf((8, 3, 2, 256), F32),
+            buf((4, 2, 4, 256), F32), buf((4, 2, 4, 256), F32),
+            buf((16, 128), BF16), buf((16, 16, 128), BF16),
+            buf((2, 3, 2, 256), F32), buf((8, 3, 2, 256), F32),
             buf((16, 256), BF16), buf((8, 16, 256), BF16),
             buf((32, 1, 128), F32), buf((64, 1, 128), F32),
             buf((2, 128), F32), buf((8, 2, 128), F32),
             buf((256, 256), BF16), buf((256, 256), BF16), buf((512, 512), BF16),
-            buf((8, 256, 256), BF16), buf((8, 256, 256), BF16),
-            buf((8, 256, 256), BF16), buf((8, 256, 256), BF16),
+            buf((8, 256, 512), BF16), buf((8, 512, 256), BF16),
             pltpu.SemaphoreType.DMA((5,)),
             pltpu.SemaphoreType.REGULAR((2,)), pltpu.SemaphoreType.DMA((8,)),
             pltpu.SemaphoreType.DMA((11,)), pltpu.SemaphoreType.DMA((11,)),

time: 69.7 us -> 68.6 us (0.984)
  Pallas kernels: 68.9 us -> 67.8 us
    pallas_call x1, Pallas kernels: 67.5 us -> 66.4 us  [per_device(): pl.pallas_call(kernel, out_shape=tuple((pltpu.VMEM(shape, kind) for shape...]
where the time goes in v6:
time: 68.6 us; the launch traced here: 68.4 us
  Pallas kernels  67.8 us (99%)
    pallas_call x1, Pallas kernels, per_device(): pl.pallas_call(kernel, out_shape=tuple((pltpu.VMEM(shape, kind) for shape...  66.4 us
    pallas_call x1, Pallas kernels, per_device(): pl.pallas_call(write_out, out_shape=tuple((pltpu.HBM(shape, kind) for sha...  1.4 us

profile of v6, /device:TPU:1, one launch (start us, length us, event | category | flops | bytes accessed | tf_op | source)
XLA Modules:
  0.0 68.4 jit_solution(2676745279499682051)
XLA Ops:
  0.6 66.4 %soft_moe_backward.1 = (bf16[256,256]{1,0:T(8,128)(2,1)S(1)}, f32[2,32]{1,0:T(2,128)S(1)}, bf16[2,2048,128]{2,1,0:T(8,128)(2,1)S(1)}, bf16[2,128,2048]{2,1,0:T(8,128)(2,1)S(1)}) custom-call(bf16[2,2048]{1,0:T(2,128)(2,1)} %bitcast.2, bf16[256,256]{1,0:T(8,128)(2,1)} %tokens_hbm.1, bf16[256,256]{1,0:T(8,128)(2,1)} %cotan_hbm.1, ...), custom_call_target="tpu_custom_call" | custom-call | tf_op jit(solution)/shard_map/soft_moe_backward/pallas_call | solution.py:384
  67.0 1.4 %write_out.1 = (bf16[256,256]{1,0:T(8,128)(2,1)}, f32[2,32]{1,0:T(2,128)}, bf16[2,2048,128]{2,1,0:T(8,128)(2,1)}, bf16[2,128,2048]{2,1,0:T(8,128)(2,1)}) custom-call(bf16[256,256]{1,0:T(8,128)(2,1)S(1)} %get-tuple-element.12.refs_0_, f32[2,32]{1,0:T(2,128)S(1)} %get-tuple-element.13.refs_1_, bf16[2,2048,128]{2,1,0:T(8,128)(2,1)S(1)} %get-tuple-element.14.refs_2_, ...), custom_call_target="tpu_custom_call" | custom-call | tf_op jit(solution)/shard_map/write_out/pallas_call | solution.py:413
